TPU v7x, 32 devices: a whole 2x2x4 slice. The times are simulated.
32 devices in a mesh: tm: 4 (over y, core), space: 8 (over z, x).
Axes of the slice: x: 2, y: 2, z: 4, core: 2. Of those that a mesh axis runs over, the one named last changes fastest.
Arguments:
- start_field: float32 [512, 512], P('space'), may hold values from -6 to 6
- guessed: float32 [16, 512, 512], P('tm', 'space'), may hold values from -6 to 6
- diffusion: float32 [512, 512], P('space'), may hold values from 0.02 to 0.3
- peclet_x: float32 [512, 512], P('space'), may hold values from -0.9 to 0.9
- peclet_y: float32 [512, 512], P('space'), may hold values from -0.9 to 0.9
- source: float32 [512, 512], P('space'), may hold values from -0.3 to 0.3
Outputs:
- corrected: float32 [16, 512, 512], P('tm', 'space')
All inputs are finite; a program needn't handle non-finite values.
Results may differ from a plain program's by a relative error of at most 0.00002.
Values sent between devices are 32-bit elements; how exact they have to be, the bound alone decides.
No kernel may reach another device: no remote copies, remote signals or barrier semaphores. Data moves between devices by JAX's collectives and lax.ppermute only.
A program may use at most 64 MiB of HBM per device.

v0:
```python
import functools

import jax
import jax.numpy as jnp
from jax import lax
from jax.experimental import pallas as pl
from jax.experimental.pallas import tpu as pltpu
from jax.sharding import PartitionSpec as P

SUBSTEPS = 4
COARSEN_ONE = 8
COARSEN_TWO = 4
LANES = 128
PAD = 8
FAR = 16
VMEM_LIMIT = 48 * 2**20


def vmem_specs(count):
    return [pl.BlockSpec(memory_space=pltpu.VMEM)] * count


def call(kernel, name, outs, scratch, flags, *arrays, cost=0):
    return pl.pallas_call(
        kernel,
        out_shape=[jax.ShapeDtypeStruct(shape, jnp.float32) for shape in outs],
        in_specs=[pl.BlockSpec(memory_space=pltpu.SMEM)] + vmem_specs(len(arrays)),
        out_specs=vmem_specs(len(outs)),
        scratch_shapes=scratch,
        name=name,
        compiler_params=pltpu.CompilerParams(vmem_limit_bytes=VMEM_LIMIT),
        cost_estimate=pl.CostEstimate(flops=cost, bytes_accessed=1 << 20, transcendentals=0),
    )(flags, *arrays)


def column_order(columns, inverse):
    blocks = columns // LANES
    grid = lax.broadcasted_iota(jnp.int32, (columns, columns), 1 if inverse else 0)
    held = lax.broadcasted_iota(jnp.int32, (columns, columns), 0 if inverse else 1)
    matches = grid == (held % LANES) * blocks + held // LANES
    return jnp.where(matches, 1.0, 0.0).astype(jnp.bfloat16)


def split_three(value):
    high = value.astype(jnp.bfloat16)
    rest = value - high.astype(jnp.float32)
    middle = rest.astype(jnp.bfloat16)
    low = (rest - middle.astype(jnp.float32)).astype(jnp.bfloat16)
    return high, middle, low


def reorder(pieces, order):
    total = jnp.dot(pieces[2][...], order, preferred_element_type=jnp.float32)
    total = total + jnp.dot(pieces[1][...], order, preferred_element_type=jnp.float32)
    return total + jnp.dot(pieces[0][...], order, preferred_element_type=jnp.float32)


def substep(source, target, coeffs, low, high, points, with_source):
    blocks = source.shape[1]
    for row in range(low, high, 8):
        here = pl.ds(row, 8)
        centre = [[source[p, j, here, :] for j in range(blocks)] for p in range(points)]
        west_end = [pltpu.roll(centre[p][blocks - 1], 1, 1) for p in range(points)]
        east_end = [pltpu.roll(centre[p][0], LANES - 1, 1) for p in range(points)]
        for j in range(blocks):
            c = [coeffs[k, j, here, :] for k in range(6 if with_source else 5)]
            for p in range(points):
                west = west_end[p] if j == 0 else centre[p][j - 1]
                east = east_end[p] if j == blocks - 1 else centre[p][j + 1]
                north = source[p, j, pl.ds(row - 1, 8), :]
                south = source[p, j, pl.ds(row + 1, 8), :]
                own = c[0] * centre[p][j]
                if with_source:
                    own = own + c[5]
                target[p, j, here, :] = (own + (c[1] * north + c[2] * south)) + (
                    c[3] * west + c[4] * east
                )


def weights(raw, offset, coeffs, rows, scale, with_source):
    blocks = coeffs.shape[1]
    lane = lax.broadcasted_iota(jnp.int32, (8, LANES), 1)
    for j in range(blocks):
        for row in range(0, rows, 8):
            rate, along, across = (raw[k, j, pl.ds(offset + row, 8), :] for k in range(3))
            inverse = 1.0 / (1.0 + 4.0 * scale * rate)
            pull = scale * rate * inverse
            west = pull * (1.0 + along)
            east = pull * (1.0 - along)
            if j == 0:
                west = jnp.where(lane == 0, 0.0, west)
            if j == blocks - 1:
                east = jnp.where(lane == LANES - 1, 0.0, east)
            here = pl.ds(PAD + row, 8)
            coeffs[0, j, here, :] = inverse
            coeffs[1, j, here, :] = pull * (1.0 + across)
            coeffs[2, j, here, :] = pull * (1.0 - across)
            coeffs[3, j, here, :] = west
            coeffs[4, j, here, :] = east
            if with_source:
                coeffs[5, j, here, :] = scale * raw[3, j, pl.ds(offset + row, 8), :] * inverse


def clear_ends(ref):
    rows = ref.shape[2]
    edge = jnp.zeros(ref.shape[:2] + (PAD, LANES), jnp.float32)
    ref[:, :, 0:PAD, :] = edge
    ref[:, :, rows - PAD : rows, :] = edge


def arrange_kernel(flags, start, guessed, rate, along, across, drive, coeffs, late, early, first, last, *parts):
    points, rows, columns = guessed.shape
    blocks = columns // LANES
    order = column_order(columns, False)
    closing = flags[2] == 1

    @pl.when(closing)
    def _():
        for part, value in zip(parts, split_three(start[...])):
            part[pl.ds(7 * rows, rows), :] = value

    @pl.when(jnp.logical_not(closing))
    def _():
        for part, value in zip(parts, split_three(guessed[points - 1])):
            part[pl.ds(7 * rows, rows), :] = value

    fields = [rate[...], along[...], across[...], drive[...]] + [guessed[k] for k in range(points - 1)]
    for index, field in enumerate(fields):
        for part, value in zip(parts, split_three(field)):
            part[pl.ds(index * rows, rows), :] = value
    result = reorder(parts, order)
    homes = [coeffs.at[k] for k in range(4)] + [early.at[0], early.at[1], late.at[0], late.at[1]]
    for index, home in enumerate(homes):
        for j in range(blocks):
            tile = result[index * rows : (index + 1) * rows, j * LANES : (j + 1) * LANES]
            home[j] = tile
            first[index, j] = tile[:FAR]
            last[index, j] = tile[rows - FAR :]


def fill_window(even, window, base, pieces, count, shift):
    own, partner, other, above, below = pieces
    rows = own.shape[2]
    top = base + FAR
    middle = top + rows
    bottom = middle + rows
    for p in range(count):
        window[p, :, pl.ds(base, FAR), :] = above[shift + p]
        window[p, :, pl.ds(middle, rows), :] = own[p]
        window[p, :, pl.ds(bottom + rows, FAR), :] = below[shift + p]

        @pl.when(even)
        def _():
            window[p, :, pl.ds(top, rows), :] = other[p]
            window[p, :, pl.ds(bottom, rows), :] = partner[p]

        @pl.when(jnp.logical_not(even))
        def _():
            window[p, :, pl.ds(top, rows), :] = partner[p]
            window[p, :, pl.ds(bottom, rows), :] = other[p]


def run_sweeps(a, b, coeffs, rows, points, snapshot):
    half = SUBSTEPS * COARSEN_ONE
    for stage in range(2 * half // 8):
        if stage == half // 8:
            snapshot()
        low = PAD + 8 * stage
        high = PAD + rows - 8 * stage

        def pair(_, carry):
            substep(a, b, coeffs, low, high, points, True)
            substep(b, a, coeffs, low, high, points, True)
            return carry

        lax.fori_loop(0, 4, pair, 0)


def late_kernel(flags, c0, c1, c2, above, below, f0, f1, f2, shift_out, settled_out, raw_out, raw, coeffs, a, b):
    even = flags[1] == 0
    rows = c0.shape[2]
    total = 3 * rows + 2 * FAR
    fill_window(even, raw, 0, (c0, c1, c2, above, below), 4, 0)
    weights(raw, 0, coeffs, total, 1.0, True)
    raw_rows = raw_out.shape[2]
    raw_out[...] = raw[0:3, :, pl.ds((total - raw_rows) // 2, raw_rows), :]
    for ref in (a, b):
        clear_ends(ref)
    fill_window(even, a, PAD, (f0, f1, f2, above, below), 2, 6)
    kept = rows + 2 * FAR
    keep = pl.ds(PAD + 2 * SUBSTEPS * COARSEN_ONE, kept)

    def snapshot():
        settled_out[...] = a[0, :, keep, :]
        shift_out[2] = a[1, :, keep, :]

    run_sweeps(a, b, coeffs, total, 2, snapshot)
    shift_out[1] = a[1, :, keep, :]

    @pl.when(flags[2] == 1)
    def _():
        shift_out[0] = shift_out[2] - shift_out[2]

    @pl.when(flags[2] == 0)
    def _():
        shift_out[0] = a[0, :, keep, :] - shift_out[2]


def early_kernel(flags, c0, c1, c2, above, below, f0, f1, f2, settled_out, swept_out, raw, coeffs, a, b):
    even = flags[1] == 0
    rows = c0.shape[2]
    total = 3 * rows + 2 * FAR
    fill_window(even, raw, 0, (c0, c1, c2, above, below), 4, 0)
    weights(raw, 0, coeffs, total, 1.0, True)
    for ref in (a, b):
        clear_ends(ref)
    fill_window(even, a, PAD, (f0, f1, f2, above, below), 2, 4)
    keep = pl.ds(PAD + 2 * SUBSTEPS * COARSEN_ONE, rows + 2 * FAR)

    def snapshot():
        settled_out[...] = a[:, :, keep, :]

    run_sweeps(a, b, coeffs, total, 2, snapshot)
    swept_out[...] = a[:, :, keep, :]


def coarse_step(a, b, coeffs, low, high, points):
    for _ in range(SUBSTEPS // 2):
        substep(a, b, coeffs, low, high, points, False)
        substep(b, a, coeffs, low, high, points, False)


def slab_kernel(flags, raw, arrived, settled, swept, settled_last, e_out, c_out, coeffs, a, b):
    kept = settled.shape[2]
    rows = kept - 2 * FAR
    weights(raw, (raw.shape[2] - kept) // 2, coeffs, kept, float(COARSEN_ONE), False)
    for ref in (a, b):
        clear_ends(ref)
    own = pl.ds(FAR, rows)
    residual = [
        lambda: arrived[0],
        lambda: arrived[1] - settled[0],
        lambda: swept[0] - settled[1],
        lambda: swept[1] - settled_last[...],
    ]
    inner = pl.ds(PAD, kept)
    a[0, :, inner, :] = residual[0]()
    e_out[0] = a[0, :, pl.ds(PAD + FAR, rows), :]
    for position in range(1, COARSEN_TWO):
        trim = 8 * ((position - 1) * SUBSTEPS // 8)
        coarse_step(a, b, coeffs, PAD + trim, PAD + kept - trim, 1)
        a[0, :, inner, :] = a[0, :, inner, :] + residual[position]()
        e_out[position] = a[0, :, pl.ds(PAD + FAR, rows), :]
    c_out[...] = e_out[COARSEN_TWO - 1]


def close_kernel(flags, raw, gathered, edges, arrived, settled, settled_last, e, out, level_coeffs, top_coeffs, a, b, w, l, x, y, *parts):
    slabs = gathered.shape[0]
    chain = slabs - 1
    rows = gathered.shape[2]
    reach = edges.shape[3]
    total = rows + 2 * reach
    offset = (raw.shape[2] - total) // 2
    weights(raw, offset, level_coeffs, total, float(COARSEN_ONE), False)
    weights(raw, offset, top_coeffs, total, float(COARSEN_ONE * COARSEN_TWO), False)
    for ref in (a, b, x, y):
        clear_ends(ref)
    for k in range(chain):
        a[k, :, pl.ds(PAD, reach), :] = edges[k, 0]
        a[k, :, pl.ds(PAD + reach, rows), :] = gathered[k]
        a[k, :, pl.ds(PAD + reach + rows, reach), :] = edges[k, 1]
    inner = pl.ds(PAD, total)
    w[0] = jnp.zeros(w.shape[1:], jnp.float32)
    l[0] = jnp.zeros(l.shape[1:], jnp.float32)
    for k in range(chain):
        w[k + 1] = a[k, :, inner, :]
    for step in range(COARSEN_TWO):
        trim = 8 * (step * SUBSTEPS // 8)
        coarse_step(a, b, level_coeffs, PAD + trim, PAD + total - trim, chain)
    used = COARSEN_TWO * SUBSTEPS
    x[0, :, inner, :] = a[0, :, inner, :]
    l[1] = x[0, :, inner, :]
    for k in range(1, chain):
        w[k + 1] = w[k + 1] + l[k]
        trim = 8 * (used // 8)
        coarse_step(x, y, top_coeffs, PAD + trim, PAD + total - trim, 1)
        used += SUBSTEPS
        x[0, :, inner, :] = x[0, :, inner, :] + a[k, :, inner, :]
        l[k + 1] = x[0, :, inner, :]
    slab = flags[0]
    own = pl.ds(reach, rows)
    held = pl.ds(PAD + reach, rows)
    x[0, :, inner, :] = w[slab]
    settled_own = pl.ds(FAR, rows)
    blocks = gathered.shape[1]
    for position in range(COARSEN_TWO):
        if position < COARSEN_TWO - 1:
            trim = 8 * ((reach - COARSEN_TWO * SUBSTEPS + SUBSTEPS * position) // 8)
            coarse_step(x, y, level_coeffs, PAD + trim, PAD + total - trim, 1)
            settled_here = arrived.at[2] if position == 0 else settled.at[position - 1]
            value = x[0, :, held, :]
        else:
            settled_here = settled_last
            value = l[slab, :, own, :]
        value = (settled_here[:, settled_own, :] + e[position]) + value
        for j in range(blocks):
            for part, piece in zip(parts, split_three(value[j])):
                part[pl.ds(position * rows, rows), j * LANES : (j + 1) * LANES] = piece
    result = reorder(parts, column_order(blocks * LANES, True))
    for position in range(COARSEN_TWO):
        out[position] = result[position * rows : (position + 1) * rows]


def on_device(start_field, guessed, diffusion, peclet_x, peclet_y, source):
    points, rows, columns = guessed.shape
    blocks = columns // LANES
    slab = lax.axis_index("tm")
    slabs = lax.axis_size("tm")
    strip = lax.axis_index("space")
    strips = lax.axis_size("space")
    flags = jnp.stack([slab, strip % 2, (slab == slabs - 1).astype(jnp.int32)]).astype(jnp.int32)

    field = (blocks, rows, LANES)
    parts = [pltpu.VMEM((8 * rows, columns), jnp.bfloat16)] * 3
    coeffs, late, early, first, last = call(
        arrange_kernel, "arrange",
        [(4,) + field, (2,) + field, (2,) + field, (8, blocks, FAR, LANES), (8, blocks, FAR, LANES)],
        parts, flags, start_field, guessed, diffusion, peclet_x, peclet_y, source,
    )
    swap = [(i, i ^ 1) for i in range(strips)]
    up = [(i, i + 2) for i in range(strips - 2)]
    down = [(i + 2, i) for i in range(strips - 2)]
    onward = [(i, i + 2) for i in range(0, strips - 2, 2)] + [(i, i - 2) for i in range(3, strips, 2)]

    above = lax.ppermute(last, "space", up)
    below = lax.ppermute(first, "space", down)
    coeffs_partner = lax.ppermute(coeffs, "space", swap)
    late_partner = lax.ppermute(late, "space", swap)
    early_partner = lax.ppermute(early, "space", swap)
    coeffs_other = lax.ppermute(coeffs_partner, "space", onward)
    late_other = lax.ppermute(late_partner, "space", onward)
    early_other = lax.ppermute(early_partner, "space", onward)

    total = 3 * rows + 2 * FAR
    kept = rows + 2 * FAR
    reach = 8 * -(-(SUBSTEPS * (2 * COARSEN_TWO - 1 + max(slabs - 3, 0))) // 8)
    spread = max(reach, FAR)
    window = (blocks, total + 2 * PAD, LANES)
    scratch = [
        pltpu.VMEM((4, blocks, total, LANES), jnp.float32),
        pltpu.VMEM((6,) + window, jnp.float32),
        pltpu.VMEM((2,) + window, jnp.float32),
        pltpu.VMEM((2,) + window, jnp.float32),
    ]
    work = 2 * SUBSTEPS * COARSEN_ONE * 2 * 10 * columns * (total - 56)
    near = (blocks, kept, LANES)
    outgoing, settled_last, raw = call(
        late_kernel, "late_points",
        [(3,) + near, near, (3, blocks, rows + 2 * spread, LANES)], scratch, flags,
        coeffs, coeffs_partner, coeffs_other, above, below, late, late_partner, late_other, cost=work,
    )
    arrived = lax.ppermute(outgoing, "tm", [(i, (i + 1) % slabs) for i in range(slabs)])
    settled, swept = call(
        early_kernel, "early_points", [(2,) + near, (2,) + near], scratch, flags,
        coeffs, coeffs_partner, coeffs_other, above, below, early, early_partner, early_other, cost=work,
    )
    padded = (blocks, kept + 2 * PAD, LANES)
    e, c_value = call(
        slab_kernel, "slab_value", [(COARSEN_TWO,) + field, field],
        [pltpu.VMEM((5,) + padded, jnp.float32)] + [pltpu.VMEM((1,) + padded, jnp.float32)] * 2,
        flags, raw, arrived, settled, swept, settled_last,
    )
    forward = [(i, i + 1) for i in range(strips - 1)]
    backward = [(i + 1, i) for i in range(strips - 1)]
    from_above = lax.ppermute(c_value[:, rows - reach :, :], "space", forward)
    from_below = lax.ppermute(c_value[:, :reach, :], "space", backward)
    gathered = lax.all_gather(c_value, "tm")
    edges = lax.all_gather(jnp.stack([from_above, from_below]), "tm")

    span = rows + 2 * reach
    wide = (blocks, span + 2 * PAD, LANES)
    plain = (slabs, blocks, span, LANES)
    out_parts = [pltpu.VMEM((COARSEN_TWO * rows, columns), jnp.bfloat16)] * 3
    (out,) = call(
        close_kernel, "close", [(COARSEN_TWO, rows, columns)],
        [pltpu.VMEM((5,) + wide, jnp.float32)] * 2
        + [pltpu.VMEM((slabs - 1,) + wide, jnp.float32)] * 2
        + [pltpu.VMEM(plain, jnp.float32)] * 2
        + [pltpu.VMEM((1,) + wide, jnp.float32)] * 2
        + out_parts,
        flags, raw, gathered, edges, arrived, settled, settled_last, e,
    )
    return out


def solution(mesh):
    in_specs = (
        P("space", None),
        P("tm", "space", None),
        P("space", None),
        P("space", None),
        P("space", None),
        P("space", None),
    )
    out_specs = P("tm", "space", None)
    return jax.shard_map(
        on_device, mesh=mesh, in_specs=in_specs, out_specs=out_specs, check_vma=False
    )
```

profile of v0, /device:TPU:25, one launch (start us, length us, event | category | flops | bytes accessed | tf_op | source)
XLA Modules:
  0.0 135.9 jit_solution(14261604904143877107)
XLA Ops:
  0.0 0.1 pad_add_fusion.flags
  0.1 0.0 copy-start
  0.1 1.0 copy-done
  1.1 0.0 copy-start.1
  1.1 0.9 copy-done.1
  2.0 0.0 copy-start.2
  2.0 0.9 copy-done.2
  2.9 0.0 copy-start.3
  2.9 0.9 copy-done.3
  3.8 0.0 copy-start.4
  3.8 0.9 copy-done.4
  4.7 0.0 copy-start.5
  4.7 0.9 copy-done.5
  5.6 1.7 %arrange.1 = (f32[4,4,64,128]{3,2,1,0:T(8,128)S(1)}, f32[2,4,64,128]{3,2,1,0:T(8,128)S(1)}, f32[2,4,64,128]{3,2,1,0:T(8,128)S(1)}, f32[8,4,16,128]{3,2,1,0:T(8,128)S(1)}, f32[8,4,16,128]{3,2,1,0:T(8,128)S(1)}) custom-call(s32[3]{0:T(128)S(1)} %pad_add_fusion.flags, f32[64,512]{1,0:T(8,128)S(1)} %copy-done.1, f32[4,64,512]{2,1,0:T(8,128)S(1)} %copy-done, ...), custom_call_target="tpu_custom_call" | custom-call | bytes 1048576 | tf_op jit(solution)/shard_map/arrange/pallas_call | solution.py:24
  7.4 1.3 collective-permute-start
  8.7 0.3 collective-permute-start.4
  8.9 11.3 %collective-permute-done.c1 = f32[4,4,64,128]{3,2,1,0:T(8,128)S(1)} collective-permute-done((f32[4,4,64,128]{3,2,1,0:T(8,128)S(1)}, f32[4,4,64,128]{3,2,1,0:T(8,128)S(1)}, u32[]{:S(2)}, u32[]{:S(2)}) %collective-permute-start) | collective-permute-done | bytes 524320 | tf_op jit(solution)/shard_map/ppermute | solution.py:337
  20.2 1.3 collective-permute-start.1
  21.5 1.3 collective-permute-start.2
  22.8 4.6 %collective-permute-start.3 = (f32[8,4,16,128]{3,2,1,0:T(8,128)S(1)}, f32[8,4,16,128]{3,2,1,0:T(8,128)S(1)}, u32[]{:S(2)}, u32[]{:S(2)}) collective-permute-start(f32[8,4,16,128]{3,2,1,0:T(8,128)S(1)} %get-tuple-element.19), channel_id=1, source_target_pairs={{2,0},{3,1},{4,2},{5,3},{6,4},{7,5},{10,8},{11,9},{12,10},{13,11},... | collective-permute-start | bytes 786440 | tf_op jit(solution)/shard_map/ppermute | solution.py:336
  27.5 0.0 collective-permute-done.4.f1
  27.5 1.3 collective-permute-start.5
  28.8 9.7 %collective-permute-done.2.above = f32[8,4,16,128]{3,2,1,0:T(8,128)S(1)} collective-permute-done((f32[8,4,16,128]{3,2,1,0:T(8,128)S(1)}, f32[8,4,16,128]{3,2,1,0:T(8,128)S(1)}, u32[]{:S(2)}, u32[]{:S(2)}) %collective-permute-start.2) | collective-permute-done | bytes 262176 | tf_op jit(solution)/shard_map/ppermute | solution.py:335
  38.5 0.0 collective-permute-done.3.below
  38.5 5.6 %collective-permute-done.5.f2 = f32[2,4,64,128]{3,2,1,0:T(8,128)S(1)} collective-permute-done((f32[2,4,64,128]{3,2,1,0:T(8,128)S(1)}, f32[2,4,64,128]{3,2,1,0:T(8,128)S(1)}, u32[]{:S(2)}, u32[]{:S(2)}) %collective-permute-start.5) | collective-permute-done | bytes 262176 | tf_op jit(solution)/shard_map/ppermute | solution.py:341
  44.1 0.0 collective-permute-done.1.c2
  44.1 18.8 %late_points.1 = (f32[3,4,96,128]{3,2,1,0:T(8,128)S(1)}, f32[4,96,128]{2,1,0:T(8,128)S(1)}, f32[3,4,128,128]{3,2,1,0:T(8,128)S(1)}) custom-call(s32[3]{0:T(128)S(1)} %pad_add_fusion.flags, f32[4,4,64,128]{3,2,1,0:T(8,128)S(1)} %get-tuple-element.17.c0, f32[4,4,64,128]{3,2,1,0:T(8,128)S(1)} %collective-permute-done.c1, ...), custom_call_target="tpu_custom_call" | custom-call | flops 110100480 | bytes 1048576 | tf_op jit(solution)/shard_map/late_points/pallas_call | solution.py:24
  62.8 4.8 %collective-permute-start.6 = (f32[3,4,96,128]{3,2,1,0:T(8,128)S(1)}, f32[3,4,96,128]{3,2,1,0:T(8,128)S(1)}, u32[]{:S(2)}, u32[]{:S(2)}) collective-permute-start(f32[3,4,96,128]{3,2,1,0:T(8,128)S(1)} %get-tuple-element.22), channel_id=1, source_target_pairs={{0,8},{8,16},{16,24},{24,0},{1,9},{9,17},{17,25},{25,1},{2,10},{10... | collective-permute-start | bytes 1769480 | tf_op jit(solution)/shard_map/ppermute | solution.py:362
  67.6 0.0 collective-permute-start.7
  67.6 7.7 %collective-permute-done.7.f1 = f32[2,4,64,128]{3,2,1,0:T(8,128)S(1)} collective-permute-done((f32[2,4,64,128]{3,2,1,0:T(8,128)S(1)}, f32[2,4,64,128]{3,2,1,0:T(8,128)S(1)}, u32[]{:S(2)}, u32[]{:S(2)}) %collective-permute-start.7) | collective-permute-done | bytes 262176 | tf_op jit(solution)/shard_map/ppermute | solution.py:339
  75.4 1.3 collective-permute-start.8
  76.7 8.6 %collective-permute-done.8.f2 = f32[2,4,64,128]{3,2,1,0:T(8,128)S(1)} collective-permute-done((f32[2,4,64,128]{3,2,1,0:T(8,128)S(1)}, f32[2,4,64,128]{3,2,1,0:T(8,128)S(1)}, u32[]{:S(2)}, u32[]{:S(2)}) %collective-permute-start.8) | collective-permute-done | bytes 262176 | tf_op jit(solution)/shard_map/ppermute | solution.py:342
  85.2 18.9 %early_points.1 = (f32[2,4,96,128]{3,2,1,0:T(8,128)S(1)}, f32[2,4,96,128]{3,2,1,0:T(8,128)S(1)}) custom-call(s32[3]{0:T(128)S(1)} %pad_add_fusion.flags, f32[4,4,64,128]{3,2,1,0:T(8,128)S(1)} %get-tuple-element.17.c0, f32[4,4,64,128]{3,2,1,0:T(8,128)S(1)} %collective-permute-done.c1, f32[4,4,64,128]{3,2,1,0:T(8,128)S(1)} %collective-permute-done.1.c2, ...), custom_call_target="tpu_custom_call" | custom-call | flops 110100480 | bytes 1048576 | tf_op jit(solution)/shard_map/early_points/pallas_call | solution.py:24
  104.1 0.0 collective-permute-done.6.arrived
  104.1 1.7 %slab_value.1 = (f32[4,4,64,128]{3,2,1,0:T(8,128)S(1)}, f32[4,64,128]{2,1,0:T(8,128)S(1)}) custom-call(s32[3]{0:T(128)S(1)} %pad_add_fusion.flags, f32[3,4,128,128]{3,2,1,0:T(8,128)S(1)} %get-tuple-element.21.raw, f32[3,4,96,128]{3,2,1,0:T(8,128)S(1)} %collective-permute-done.6.arrived, f32[2,4,96,128]{3,2,1,0:T(8,128)S(1)} %get-tuple-element.24.settled, ...), custom_call_target="tpu_custom_call" | custom-call | bytes 1048576 | tf_op jit(solution)/shard_map/slab_value/pallas_call | solution.py:24
  105.8 1.9 %collective-permute-start.9 = (f32[4,32,128]{2,1,0:T(8,128)S(1)}, f32[4,32,128]{2,1,0:T(8,128)S(1)}, u32[]{:S(2)}, u32[]{:S(2)}) collective-permute-start(f32[4,32,128]{2,1,0:T(8,128)S(1)} %get-tuple-element.29), channel_id=1, source_target_pairs={{0,1},{1,2},{2,3},{3,4},{4,5},{5,6},{6,7},{8,9},{9,10},{10,11},{11... | collective-permute-start | bytes 196616 | tf_op jit(solution)/shard_map/ppermute | solution.py:375
  107.8 4.3 %collective-permute-start.10 = (f32[4,32,128]{2,1,0:T(8,128)S(1)}, f32[4,32,128]{2,1,0:T(8,128)S(1)}, u32[]{:S(2)}, u32[]{:S(2)}) collective-permute-start(f32[4,32,128]{2,1,0:T(8,128)S(1)} %get-tuple-element.30), channel_id=1, source_target_pairs={{1,0},{2,1},{3,2},{4,3},{5,4},{6,5},{7,6},{9,8},{10,9},{11,10},{12... | collective-permute-start | bytes 196616 | tf_op jit(solution)/shard_map/ppermute | solution.py:376
  112.0 7.6 %all-gather = f32[16,64,128]{2,1,0:T(8,128)S(1)} all-gather(f32[4,64,128]{2,1,0:T(8,128)S(1)} %get-tuple-element.27), channel_id=2, replica_groups=mesh['tm'=4,'space'=8] {'tm'}, dimensions={0}, use_global_device_ids=true | all-gather | bytes 655360 | tf_op jit(solution)/shard_map/all_gather | solution.py:377
  119.7 0.0 collective-permute-done.9
  119.7 0.0 collective-permute-done.10
  119.7 7.5 %all-gather.1 = f32[8,4,32,128]{3,2,1,0:T(8,128)S(1)} all-gather(f32[2,4,32,128]{3,2,1,0:T(8,128)S(1)} %pad_maximum_fusion), channel_id=3, replica_groups=mesh['tm'=4,'space'=8] {'tm'}, dimensions={0}, use_global_device_ids=true | all-gather | bytes 655360 | tf_op jit(solution)/shard_map/all_gather | solution.py:378
  127.2 8.6 %close.1 = f32[4,64,512]{2,1,0:T(8,128)} custom-call(s32[3]{0:T(128)S(1)} %pad_add_fusion.flags, f32[3,4,128,128]{3,2,1,0:T(8,128)S(1)} %get-tuple-element.21.raw, f32[4,4,64,128]{3,2,1,0:T(8,128)S(1)} %bitcast.7, f32[4,2,4,32,128]{4,3,2,1,0:T(8,128)S(1)} %bitcast.8, f32[3,4,96,128]{3,2,1,0:T(8,128)S(1)} %collective-permute-done.6.arrived, ...), custom_call_target="tpu_custom_call" | custom-call | bytes 1048576 | tf_op jit(solution)/shard_map/close/pallas_call | solution.py:24
  (2 shorter events, 0.0 us)
Async XLA Ops:
  0.1 1.0 copy-start
  1.1 0.9 copy-start.1
  2.0 0.9 copy-start.2
  2.9 0.9 copy-start.3
  3.8 0.9 copy-start.4
  4.7 0.9 copy-start.5
  7.4 12.9 %collective-permute-start = (f32[4,4,64,128]{3,2,1,0:T(8,128)S(1)}, f32[4,4,64,128]{3,2,1,0:T(8,128)S(1)}, u32[]{:S(2)}, u32[]{:S(2)}) collective-permute-start(f32[4,4,64,128]{3,2,1,0:T(8,128)S(1)} %get-tuple-element.17.c0), channel_id=1, source_target_pairs={{0,1},{1,0},{2,3},{3,2},{4,5},{5,4},{6,7},{7,6},{8,9},{9,8},{10,11... | collective-permute-start | bytes 1572872 | tf_op jit(solution)/shard_map/ppermute | solution.py:337
  8.7 18.8 %collective-permute-start.4 = (f32[2,4,64,128]{3,2,1,0:T(8,128)S(1)}, f32[2,4,64,128]{3,2,1,0:T(8,128)S(1)}, u32[]{:S(2)}, u32[]{:S(2)}) collective-permute-start(f32[2,4,64,128]{3,2,1,0:T(8,128)S(1)} %get-tuple-element.20.f0), channel_id=1, source_target_pairs={{0,1},{1,0},{2,3},{3,2},{4,5},{5,4},{6,7},{7,6},{8,9},{9,8},{10,11... | collective-permute-start | bytes 786440 | tf_op jit(solution)/shard_map/ppermute | solution.py:338
  20.2 23.8 %collective-permute-start.1 = (f32[4,4,64,128]{3,2,1,0:T(8,128)S(1)}, f32[4,4,64,128]{3,2,1,0:T(8,128)S(1)}, u32[]{:S(2)}, u32[]{:S(2)}) collective-permute-start(f32[4,4,64,128]{3,2,1,0:T(8,128)S(1)} %collective-permute-done.c1), channel_id=1, source_target_pairs={{0,2},{2,4},{4,6},{3,1},{5,3},{7,5},{8,10},{10,12},{12,14},{11,9},... | collective-permute-start | bytes 1572872 | tf_op jit(solution)/shard_map/ppermute | solution.py:340
  21.5 16.9 %collective-permute-start.2 = (f32[8,4,16,128]{3,2,1,0:T(8,128)S(1)}, f32[8,4,16,128]{3,2,1,0:T(8,128)S(1)}, u32[]{:S(2)}, u32[]{:S(2)}) collective-permute-start(f32[8,4,16,128]{3,2,1,0:T(8,128)S(1)} %get-tuple-element.18), channel_id=1, source_target_pairs={{0,2},{1,3},{2,4},{3,5},{4,6},{5,7},{8,10},{9,11},{10,12},{11,13},... | collective-permute-start | bytes 786440 | tf_op jit(solution)/shard_map/ppermute | solution.py:335
  22.8 15.6 %collective-permute-start.3 = (f32[8,4,16,128]{3,2,1,0:T(8,128)S(1)}, f32[8,4,16,128]{3,2,1,0:T(8,128)S(1)}, u32[]{:S(2)}, u32[]{:S(2)}) collective-permute-start(f32[8,4,16,128]{3,2,1,0:T(8,128)S(1)} %get-tuple-element.19), channel_id=1, source_target_pairs={{2,0},{3,1},{4,2},{5,3},{6,4},{7,5},{10,8},{11,9},{12,10},{13,11},... | collective-permute-start | bytes 786440 | tf_op jit(solution)/shard_map/ppermute | solution.py:336
  27.5 16.6 %collective-permute-start.5 = (f32[2,4,64,128]{3,2,1,0:T(8,128)S(1)}, f32[2,4,64,128]{3,2,1,0:T(8,128)S(1)}, u32[]{:S(2)}, u32[]{:S(2)}) collective-permute-start(f32[2,4,64,128]{3,2,1,0:T(8,128)S(1)} %collective-permute-done.4.f1), channel_id=1, source_target_pairs={{0,2},{2,4},{4,6},{3,1},{5,3},{7,5},{8,10},{10,12},{12,14},{11,9},... | collective-permute-start | bytes 786440 | tf_op jit(solution)/shard_map/ppermute | solution.py:341
  62.8 41.3 %collective-permute-start.6 = (f32[3,4,96,128]{3,2,1,0:T(8,128)S(1)}, f32[3,4,96,128]{3,2,1,0:T(8,128)S(1)}, u32[]{:S(2)}, u32[]{:S(2)}) collective-permute-start(f32[3,4,96,128]{3,2,1,0:T(8,128)S(1)} %get-tuple-element.22), channel_id=1, source_target_pairs={{0,8},{8,16},{16,24},{24,0},{1,9},{9,17},{17,25},{25,1},{2,10},{10... | collective-permute-start | bytes 1769480 | tf_op jit(solution)/shard_map/ppermute | solution.py:362
  67.6 7.7 %collective-permute-start.7 = (f32[2,4,64,128]{3,2,1,0:T(8,128)S(1)}, f32[2,4,64,128]{3,2,1,0:T(8,128)S(1)}, u32[]{:S(2)}, u32[]{:S(2)}) collective-permute-start(f32[2,4,64,128]{3,2,1,0:T(8,128)S(1)} %get-tuple-element.23.f0), channel_id=1, source_target_pairs={{0,1},{1,0},{2,3},{3,2},{4,5},{5,4},{6,7},{7,6},{8,9},{9,8},{10,11... | collective-permute-start | bytes 786440 | tf_op jit(solution)/shard_map/ppermute | solution.py:339
  75.4 9.9 %collective-permute-start.8 = (f32[2,4,64,128]{3,2,1,0:T(8,128)S(1)}, f32[2,4,64,128]{3,2,1,0:T(8,128)S(1)}, u32[]{:S(2)}, u32[]{:S(2)}) collective-permute-start(f32[2,4,64,128]{3,2,1,0:T(8,128)S(1)} %collective-permute-done.7.f1), channel_id=1, source_target_pairs={{0,2},{2,4},{4,6},{3,1},{5,3},{7,5},{8,10},{10,12},{12,14},{11,9},... | collective-permute-start | bytes 786440 | tf_op jit(solution)/shard_map/ppermute | solution.py:342
  105.8 13.8 %collective-permute-start.9 = (f32[4,32,128]{2,1,0:T(8,128)S(1)}, f32[4,32,128]{2,1,0:T(8,128)S(1)}, u32[]{:S(2)}, u32[]{:S(2)}) collective-permute-start(f32[4,32,128]{2,1,0:T(8,128)S(1)} %get-tuple-element.29), channel_id=1, source_target_pairs={{0,1},{1,2},{2,3},{3,4},{4,5},{5,6},{6,7},{8,9},{9,10},{10,11},{11... | collective-permute-start | bytes 196616 | tf_op jit(solution)/shard_map/ppermute | solution.py:375
  107.8 11.9 %collective-permute-start.10 = (f32[4,32,128]{2,1,0:T(8,128)S(1)}, f32[4,32,128]{2,1,0:T(8,128)S(1)}, u32[]{:S(2)}, u32[]{:S(2)}) collective-permute-start(f32[4,32,128]{2,1,0:T(8,128)S(1)} %get-tuple-element.30), channel_id=1, source_target_pairs={{1,0},{2,1},{3,2},{4,3},{5,4},{6,5},{7,6},{9,8},{10,9},{11,10},{12... | collective-permute-start | bytes 196616 | tf_op jit(solution)/shard_map/ppermute | solution.py:376
where the time goes:
time: 136 us
  Pallas kernels  49.7 us (37%)
  waiting for transfers between devices  43 us (32%)
  starting transfers between devices  22.3 us (16%)
  blocking collectives  15.2 us (11%)
  local copies, waits for them, and re-layouts  5.57 us (4%)
    pallas_call x5, Pallas kernels, call(): pl.pallas_call(kernel, out_shape=[jax.ShapeDtypeStruct(shape, jnp.float32...  49.7 us
    ppermute x1, waiting for transfers between devices, on_device(): coeffs_partner = lax.ppermute(coeffs, 'space', swap)  11.3 us
    ppermute x1, waiting for transfers between devices, on_device(): above = lax.ppermute(last, 'space', up)  9.69 us
    ppermute x1, waiting for transfers between devices, on_device(): early_other = lax.ppermute(early_partner, 'space', onward)  8.59 us
    ppermute x1, waiting for transfers between devices, on_device(): early_partner = lax.ppermute(early, 'space', swap)  7.74 us
    all_gather x1, blocking collectives, on_device(): gathered = lax.all_gather(c_value, 'tm')  7.64 us
    all_gather x1, blocking collectives, on_device(): edges = lax.all_gather(jnp.stack([from_above, from_below]), 'tm')  7.51 us
    ppermute x1, waiting for transfers between devices, on_device(): late_other = lax.ppermute(late_partner, 'space', onward)  5.61 us
  transfers between devices with their start and end apart: 11, of which 5 were waited for; matrix products, arithmetic and copies ran while one was open for 0% of the time, Pallas kernels for 14%

commit v1 on v0

v1 whole, which is shorter than its diff:
```python
import functools

import jax
import jax.numpy as jnp
from jax import lax
from jax.experimental import pallas as pl
from jax.experimental.pallas import tpu as pltpu
from jax.sharding import PartitionSpec as P

SUBSTEPS = 4
COARSEN_ONE = 8
COARSEN_TWO = 4
LANES = 128
PAD = 8
NEAR = 16
FINE = SUBSTEPS * COARSEN_ONE
VMEM_LIMIT = 24 * 2**20


def is_last_slab():
    return lax.axis_index("tm") == lax.axis_size("tm") - 1


def vmem_specs(count):
    return [pl.BlockSpec(memory_space=pltpu.VMEM)] * count


def call(kernel, name, outs, scratch, *arrays, cost=0, far=False, grant=VMEM_LIMIT):
    held = [pl.BlockSpec(memory_space=pltpu.HBM)] * len(arrays) if far else vmem_specs(len(arrays))
    return pl.pallas_call(
        kernel,
        out_shape=[jax.ShapeDtypeStruct(shape, jnp.float32) for shape in outs],
        in_specs=held,
        out_specs=vmem_specs(len(outs)),
        scratch_shapes=scratch,
        name=name,
        compiler_params=pltpu.CompilerParams(vmem_limit_bytes=grant),
        cost_estimate=pl.CostEstimate(flops=cost, bytes_accessed=1 << 20, transcendentals=0),
    )(*arrays)


def column_order(columns, inverse):
    blocks = columns // LANES
    grid = lax.broadcasted_iota(jnp.int32, (columns, columns), 1 if inverse else 0)
    held = lax.broadcasted_iota(jnp.int32, (columns, columns), 0 if inverse else 1)
    matches = grid == (held % LANES) * blocks + held // LANES
    return jnp.where(matches, 1.0, 0.0).astype(jnp.bfloat16)


def split_three(value):
    high = value.astype(jnp.bfloat16)
    rest = value - high.astype(jnp.float32)
    middle = rest.astype(jnp.bfloat16)
    low = (rest - middle.astype(jnp.float32)).astype(jnp.bfloat16)
    return high, middle, low


def reorder(pieces, order):
    total = jnp.dot(pieces[2][...], order, preferred_element_type=jnp.float32)
    total = total + jnp.dot(pieces[1][...], order, preferred_element_type=jnp.float32)
    return total + jnp.dot(pieces[0][...], order, preferred_element_type=jnp.float32)


def substep(source, target, coeffs, low, high, points, with_source):
    blocks = source.shape[1]
    for row in range(low, high, 8):
        here = pl.ds(row, 8)
        centre = [[source[p, j, here, :] for j in range(blocks)] for p in range(points)]
        west_end = [pltpu.roll(centre[p][blocks - 1], 1, 1) for p in range(points)]
        east_end = [pltpu.roll(centre[p][0], LANES - 1, 1) for p in range(points)]
        for j in range(blocks):
            c = [coeffs[k, j, here, :] for k in range(6 if with_source else 5)]
            for p in range(points):
                west = west_end[p] if j == 0 else centre[p][j - 1]
                east = east_end[p] if j == blocks - 1 else centre[p][j + 1]
                north = source[p, j, pl.ds(row - 1, 8), :]
                south = source[p, j, pl.ds(row + 1, 8), :]
                own = c[0] * centre[p][j]
                if with_source:
                    own = own + c[5]
                target[p, j, here, :] = (own + (c[1] * north + c[2] * south)) + (
                    c[3] * west + c[4] * east
                )


def weights(raw, offset, coeffs, rows, scale, with_source):
    blocks = coeffs.shape[1]
    lane = lax.broadcasted_iota(jnp.int32, (8, LANES), 1)
    for j in range(blocks):
        for row in range(0, rows, 8):
            rate, along, across = (raw[k, j, pl.ds(offset + row, 8), :] for k in range(3))
            inverse = 1.0 / (1.0 + 4.0 * scale * rate)
            pull = scale * rate * inverse
            west = pull * (1.0 + along)
            east = pull * (1.0 - along)
            if j == 0:
                west = jnp.where(lane == 0, 0.0, west)
            if j == blocks - 1:
                east = jnp.where(lane == LANES - 1, 0.0, east)
            here = pl.ds(PAD + row, 8)
            coeffs[0, j, here, :] = inverse
            coeffs[1, j, here, :] = pull * (1.0 + across)
            coeffs[2, j, here, :] = pull * (1.0 - across)
            coeffs[3, j, here, :] = west
            coeffs[4, j, here, :] = east
            if with_source:
                coeffs[5, j, here, :] = scale * raw[3, j, pl.ds(offset + row, 8), :] * inverse


def clear_ends(ref):
    rows = ref.shape[2]
    edge = jnp.zeros(ref.shape[:2] + (PAD, LANES), jnp.float32)
    ref[:, :, 0:PAD, :] = edge
    ref[:, :, rows - PAD : rows, :] = edge


def sides(source, near, far):
    even = lax.axis_index("space") % 2 == 0
    rows = source.shape[-2]
    width = near.shape[-2]
    low = pl.multiple_of(jnp.where(even, rows - width, 0), 8)
    high = pl.multiple_of(jnp.where(even, 0, rows - width), 8)
    for k in range(near.shape[0]):
        near[k] = source[k, :, pl.ds(low, width), :]
        far[k] = source[k, :, pl.ds(high, width), :]


def arrange_kernel(
    start, guessed, rate, along, across, drive,
    coeffs, late, early, share_near, share_far, late_near, late_far, early_near, early_far,
    landed, arrivals, *parts,
):
    points, rows, columns = guessed.shape
    blocks = columns // LANES
    closing = is_last_slab()
    sources = [rate, along, across, drive] + [guessed.at[k] for k in range(points - 1)]
    copies = [
        pltpu.make_async_copy(source, landed.at[k], arrivals.at[k]) for k, source in enumerate(sources)
    ]
    final = [
        pltpu.make_async_copy(source, landed.at[7], arrivals.at[7]) for source in (start, guessed.at[points - 1])
    ]
    for copy in copies:
        copy.start()

    @pl.when(closing)
    def _():
        final[0].start()

    @pl.when(jnp.logical_not(closing))
    def _():
        final[1].start()

    order = column_order(columns, False)
    for index, copy in enumerate(copies + final[1:]):
        copy.wait()
        for part, value in zip(parts, split_three(landed[index])):
            part[pl.ds(index * rows, rows), :] = value
    result = reorder(parts, order)
    homes = [coeffs.at[k] for k in range(4)] + [early.at[0], early.at[1], late.at[0], late.at[1]]
    for index, home in enumerate(homes):
        for j in range(blocks):
            home[j] = result[index * rows : (index + 1) * rows, j * LANES : (j + 1) * LANES]
    sides(coeffs.at[pl.ds(2 * (lax.axis_index("tm") % 2), 2)], share_near, share_far)
    sides(late, late_near, late_far)
    sides(early, early_near, early_far)


def fill(window, base, own, near, far, targets):
    even = lax.axis_index("space") % 2 == 0
    rows = own.shape[2]
    width = near.shape[2]
    below = base + width + rows
    partner = pl.multiple_of(jnp.where(even, below, base), 8)
    other = pl.multiple_of(jnp.where(even, base, below), 8)
    for k, target in enumerate(targets):
        window[target, :, pl.ds(partner, width), :] = near[k]
        window[target, :, pl.ds(other, width), :] = far[k]


def run_sweep(a, b, coeffs, base, rows, points):
    for stage in range(FINE // 8):
        low = base + 8 * stage
        high = base + rows - 8 * stage

        def pairs(_, carry):
            for _ in range(2):
                substep(a, b, coeffs, low, high, points, True)
                substep(b, a, coeffs, low, high, points, True)
            return carry

        lax.fori_loop(0, 2, pairs, 0)


def load_points(a, b, own, near, far):
    points, _, rows, _ = own.shape
    width = near.shape[2]
    base = (a.shape[2] - rows) // 2 - width
    total = rows + 2 * width
    edge = jnp.zeros(a.shape[:2] + (PAD, LANES), jnp.float32)
    for ref in (a, b):
        ref[:, :, pl.ds(base - PAD, PAD), :] = edge
        ref[:, :, pl.ds(base + total, PAD), :] = edge
    for p in range(points):
        a[p, :, pl.ds(base + width, rows), :] = own[p]
    fill(a, base, own, near, far, range(points))
    return base, total


def first_sweep(coeffs, own, near, far, settled, next_near, next_far, a, b):
    base, total = load_points(a, b, own, near, far)
    run_sweep(a, b, coeffs, base, total, own.shape[0])
    settled[...] = a[:, :, pl.ds(base + FINE, own.shape[2]), :]
    sides(settled, next_near, next_far)


def open_kernel(
    mine, share_near, share_far, mates, own, near, far,
    coeffs, raw_out, settled, next_near, next_far, raw, a, b,
):
    rows = mine.shape[2]
    width = share_near.shape[2]
    total = rows + 2 * width
    for k in range(4):
        raw[k, :, pl.ds(width, rows), :] = mine[k]
    fill(raw, 0, mine, share_near, share_far, [2 * (lax.axis_index("tm") % 2) + k for k in range(2)])
    fill(raw, 0, mine, mates.at[0], mates.at[1], [2 - 2 * (lax.axis_index("tm") % 2) + k for k in range(2)])
    weights(raw, 0, coeffs, total, 1.0, True)
    clear_ends(coeffs)
    raw_rows = raw_out.shape[2]
    raw_out[...] = raw[0:3, :, pl.ds((total - raw_rows) // 2, raw_rows), :]
    first_sweep(coeffs, own, near, far, settled, next_near, next_far, a, b)


def second_sweep(coeffs, own, near, far, a, b):
    base, total = load_points(a, b, own, near, far)
    keep = pl.ds(base + FINE, total - 2 * FINE)
    return base, total, keep


def late_kernel(coeffs, own, near, far, shift_out, a, b):
    base, total, keep = second_sweep(coeffs, own, near, far, a, b)
    shift_out[2] = a[1, :, keep, :]
    run_sweep(a, b, coeffs, base, total, own.shape[0])
    shift_out[1] = a[1, :, keep, :]

    @pl.when(is_last_slab())
    def _():
        shift_out[0] = shift_out[2] - shift_out[2]

    @pl.when(jnp.logical_not(is_last_slab()))
    def _():
        shift_out[0] = a[0, :, keep, :] - shift_out[2]


def early_kernel(coeffs, own, near, far, settled_out, swept_out, a, b):
    base, total, keep = second_sweep(coeffs, own, near, far, a, b)
    settled_out[...] = a[:, :, keep, :]
    run_sweep(a, b, coeffs, base, total, own.shape[0])
    swept_out[...] = a[:, :, keep, :]


def coarse_step(a, b, coeffs, low, high, points):
    for _ in range(SUBSTEPS // 2):
        substep(a, b, coeffs, low, high, points, False)
        substep(b, a, coeffs, low, high, points, False)


def slab_kernel(raw, arrived, settled, swept, settled_last, e_out, c_out, coeffs, a, b):
    kept = settled.shape[2]
    rows = settled_last.shape[2]
    weights(raw, (raw.shape[2] - kept) // 2, coeffs, kept, float(COARSEN_ONE), False)
    for ref in (a, b):
        clear_ends(ref)
    inner = pl.ds(PAD, kept)
    own = pl.ds(NEAR, rows)
    held = pl.ds(PAD + NEAR, rows)
    a[0, :, inner, :] = arrived[0]
    e_out[0] = a[0, :, held, :]
    for position in range(1, COARSEN_TWO):
        trim = 8 * ((position - 1) * SUBSTEPS // 8)
        coarse_step(a, b, coeffs, PAD + trim, PAD + kept - trim, 1)
        if position == 1:
            a[0, :, inner, :] = a[0, :, inner, :] + (arrived[1] - settled[0])
        elif position == 2:
            a[0, :, inner, :] = a[0, :, inner, :] + (swept[0] - settled[1])
        else:
            a[0, :, held, :] = a[0, :, held, :] + (swept[1, :, own, :] - settled_last[0])
        e_out[position] = a[0, :, held, :]
    c_out[...] = e_out[COARSEN_TWO - 1]


def close_kernel(raw, gathered, edges, arrived, settled, settled_last, e, out, level_coeffs, top_coeffs, a, b, w, l, x, y, *parts):
    slabs = gathered.shape[0]
    chain = slabs - 1
    rows = gathered.shape[2]
    reach = edges.shape[3]
    total = rows + 2 * reach
    offset = (raw.shape[2] - total) // 2
    weights(raw, offset, level_coeffs, total, float(COARSEN_ONE), False)
    weights(raw, offset, top_coeffs, total, float(COARSEN_ONE * COARSEN_TWO), False)
    for ref in (a, b, x, y):
        clear_ends(ref)
    for k in range(chain):
        a[k, :, pl.ds(PAD, reach), :] = edges[k, 0]
        a[k, :, pl.ds(PAD + reach, rows), :] = gathered[k]
        a[k, :, pl.ds(PAD + reach + rows, reach), :] = edges[k, 1]
    inner = pl.ds(PAD, total)
    w[0] = jnp.zeros(w.shape[1:], jnp.float32)
    l[0] = jnp.zeros(l.shape[1:], jnp.float32)
    for k in range(chain):
        w[k + 1] = a[k, :, inner, :]
    for step in range(COARSEN_TWO):
        trim = 8 * (step * SUBSTEPS // 8)
        coarse_step(a, b, level_coeffs, PAD + trim, PAD + total - trim, chain)
    used = COARSEN_TWO * SUBSTEPS
    x[0, :, inner, :] = a[0, :, inner, :]
    l[1] = x[0, :, inner, :]
    for k in range(1, chain):
        w[k + 1] = w[k + 1] + l[k]
        trim = 8 * (used // 8)
        coarse_step(x, y, top_coeffs, PAD + trim, PAD + total - trim, 1)
        used += SUBSTEPS
        x[0, :, inner, :] = x[0, :, inner, :] + a[k, :, inner, :]
        l[k + 1] = x[0, :, inner, :]
    slab = lax.axis_index("tm")
    own = pl.ds(reach, rows)
    held = pl.ds(PAD + reach, rows)
    x[0, :, inner, :] = w[slab]
    blocks = gathered.shape[1]
    for position in range(COARSEN_TWO):
        if position < COARSEN_TWO - 1:
            trim = 8 * ((reach - COARSEN_TWO * SUBSTEPS + SUBSTEPS * position) // 8)
            coarse_step(x, y, level_coeffs, PAD + trim, PAD + total - trim, 1)
            settled_here = (arrived.at[2] if position == 0 else settled.at[position - 1]).at[:, pl.ds(NEAR, rows), :]
            value = x[0, :, held, :]
        else:
            settled_here = settled_last.at[0]
            value = l[slab, :, own, :]
        value = (settled_here[...] + e[position]) + value
        for j in range(blocks):
            for part, piece in zip(parts, split_three(value[j])):
                part[pl.ds(position * rows, rows), j * LANES : (j + 1) * LANES] = piece
    result = reorder(parts, column_order(blocks * LANES, True))
    for position in range(COARSEN_TWO):
        out[position] = result[position * rows : (position + 1) * rows]


def on_device(start_field, guessed, diffusion, peclet_x, peclet_y, source):
    points, rows, columns = guessed.shape
    blocks = columns // LANES
    slabs = lax.axis_size("tm")
    strips = lax.axis_size("space")

    field = (blocks, rows, LANES)
    parts = [pltpu.VMEM((8 * rows, columns), jnp.bfloat16)] * 3
    landing = [pltpu.VMEM((8, rows, columns), jnp.float32), pltpu.SemaphoreType.DMA((8,))]
    wide_field = (blocks, FINE + NEAR, LANES)
    halo = (blocks, FINE, LANES)
    coeffs, late, early, share_near, share_far, late_near, late_far, early_near, early_far = call(
        arrange_kernel, "arrange",
        [(4,) + field, (2,) + field, (2,) + field] + [(2,) + wide_field] * 2 + [(2,) + halo] * 4,
        landing + parts, start_field, guessed, diffusion, peclet_x, peclet_y, source, far=True, grant=61 * 2**20,
    )
    swap = [(i, i ^ 1) for i in range(strips)]
    cross = [(i, i + 1) for i in range(1, strips - 1, 2)] + [(i + 1, i) for i in range(1, strips - 1, 2)]
    mate = [(i, i ^ 1) for i in range(slabs)]

    def send(name, value, axis, route):
        with jax.named_scope(name):
            return lax.ppermute(value, axis, route)

    def exchange(name, near, far):
        return send(name + "_near", near, "space", swap), send(name + "_far", far, "space", cross)

    share_sides = exchange("share", share_near, share_far)
    late_sides = exchange("late", late_near, late_far)
    mates = send("mates", jnp.stack(share_sides), "tm", mate)
    early_sides = exchange("early", early_near, early_far)

    reach = 8 * -(-(SUBSTEPS * (2 * COARSEN_TWO - 1 + max(slabs - 3, 0))) // 8)
    spread = max(reach, NEAR)
    total = rows + 2 * (FINE + NEAR)
    window = (blocks, total + 2 * PAD, LANES)
    pair = [pltpu.VMEM((2,) + window, jnp.float32)] * 2
    work = 6 * 10**9
    near = (2, blocks, rows + 2 * NEAR, LANES)
    sent = [(2,) + field] + [(2,) + wide_field] * 2
    fine, raw, late_settled, late_near, late_far = call(
        open_kernel, "late_first_sweep",
        [(6,) + window, (3, blocks, rows + 2 * spread, LANES)] + sent,
        [pltpu.VMEM((4, blocks, total, LANES), jnp.float32)] + pair,
        coeffs, *share_sides, mates, late, *late_sides, cost=work,
    )
    late_sides = exchange("late_settled", late_near, late_far)
    early_settled, early_near, early_far = call(
        first_sweep, "early_first_sweep", sent, pair, fine, early, *early_sides, cost=work
    )
    early_sides = exchange("early_settled", early_near, early_far)
    (outgoing,) = call(
        late_kernel, "late_second_sweep", [(3,) + near[1:]], pair, fine, late_settled, *late_sides, cost=work
    )
    arrived = send("next_slab", outgoing, "tm", [(i, (i + 1) % slabs) for i in range(slabs)])
    settled, swept = call(
        early_kernel, "early_second_sweep", [near, near], pair, fine, early_settled, *early_sides, cost=work
    )
    padded = (blocks, rows + 2 * NEAR + 2 * PAD, LANES)
    e, c_value = call(
        slab_kernel, "slab_value", [(COARSEN_TWO,) + field, field],
        [pltpu.VMEM((5,) + padded, jnp.float32)] + [pltpu.VMEM((1,) + padded, jnp.float32)] * 2,
        raw, arrived, settled, swept, late_settled,
    )
    forward = [(i, i + 1) for i in range(strips - 1)]
    backward = [(i + 1, i) for i in range(strips - 1)]
    from_above = send("slab_down", c_value[:, rows - reach :, :], "space", forward)
    from_below = send("slab_up", c_value[:, :reach, :], "space", backward)
    gathered = lax.all_gather(c_value, "tm")
    edges = lax.all_gather(jnp.stack([from_above, from_below]), "tm")

    span = rows + 2 * reach
    wide = (blocks, span + 2 * PAD, LANES)
    plain = (slabs, blocks, span, LANES)
    out_parts = [pltpu.VMEM((COARSEN_TWO * rows, columns), jnp.bfloat16)] * 3
    (out,) = call(
        close_kernel, "close", [(COARSEN_TWO, rows, columns)],
        [pltpu.VMEM((5,) + wide, jnp.float32)] * 2
        + [pltpu.VMEM((slabs - 1,) + wide, jnp.float32)] * 2
        + [pltpu.VMEM(plain, jnp.float32)] * 2
        + [pltpu.VMEM((1,) + wide, jnp.float32)] * 2
        + out_parts,
        raw, gathered, edges, arrived, settled, late_settled, e,
    )
    return out


def solution(mesh):
    in_specs = (
        P("space", None),
        P("tm", "space", None),
        P("space", None),
        P("space", None),
        P("space", None),
        P("space", None),
    )
    out_specs = P("tm", "space", None)
    return jax.shard_map(
        on_device, mesh=mesh, in_specs=in_specs, out_specs=out_specs, check_vma=False
    )
```

time: 136 us -> 93.5 us (0.69)
  waiting for transfers between devices: 43 us -> 8.01 us
  Pallas kernels: 49.7 us -> 37 us
  starting transfers between devices: 22.3 us -> 29.4 us
  local copies, waits for them, and re-layouts: 5.57 us -> 2.01 us
    ppermute x11 -> x14, waiting for transfers between devices: 43 us -> 8.01 us  [send(): return lax.ppermute(value, axis, route)]
    pallas_call x5 -> x7, Pallas kernels: 49.7 us -> 37 us  [call(): pl.pallas_call(kernel, out_shape=[jax.ShapeDtypeStruct(shape, jnp.float32...]
    ppermute x11 -> x14, starting transfers between devices: 22.3 us -> 29.4 us  [send(): return lax.ppermute(value, axis, route)]
    unnamed x12 -> x6, local copies, waits for them, and re-layouts: 5.56 us -> 2 us
  transfers between devices with their start and end apart: 11 -> 14, of which waited for: 5 -> 3; matrix products, arithmetic and copies ran while one was open for 0% -> 0% of each run, Pallas kernels for 14% -> 26%
where the time goes in v1:
time: 93.5 us; the launch traced here: 92.7 us
  Pallas kernels  37 us (40%)
  starting transfers between devices  29.4 us (31%)
  blocking collectives  16.1 us (17%)
  waiting for transfers between devices  8.01 us (9%)
  local copies, waits for them, and re-layouts  2.01 us (2%)
    pallas_call x7, Pallas kernels, call(): pl.pallas_call(kernel, out_shape=[jax.ShapeDtypeStruct(shape, jnp.float32...  37 us
    ppermute x14, starting transfers between devices, send(): return lax.ppermute(value, axis, route)  29.4 us
    all_gather x1, blocking collectives, on_device(): gathered = lax.all_gather(c_value, 'tm')  8.76 us
    ppermute x14, waiting for transfers between devices, send(): return lax.ppermute(value, axis, route)  8.01 us
    all_gather x1, blocking collectives, on_device(): edges = lax.all_gather(jnp.stack([from_above, from_below]), 'tm')  7.29 us
    unnamed x6, local copies, waits for them, and re-layouts  2 us
  transfers between devices with their start and end apart: 14, of which 3 were waited for; matrix products, arithmetic and copies ran while one was open for 0% of the time, Pallas kernels for 26%

profile of v1, /device:TPU:25, one launch (start us, length us, event | category | flops | bytes accessed | tf_op | source)
XLA Modules:
  0.0 92.7 jit_solution(8257469488764160878)
XLA Ops:
  0.0 3.5 %arrange.1 = (f32[4,4,64,128]{3,2,1,0:T(8,128)}, f32[2,4,64,128]{3,2,1,0:T(8,128)}, f32[2,4,64,128]{3,2,1,0:T(8,128)}, f32[2,4,48,128]{3,2,1,0:T(8,128)}, f32[2,...) custom-call(f32[64,512]{1,0:T(8,128)} %start.1, ...), custom_call_target="tpu_custom_call" | custom-call | bytes 1048576 | tf_op jit(solution)/shard_map/arrange/pallas_call | solution.py:30
  3.5 1.3 %collective-permute-start = (f32[2,4,48,128]{3,2,1,0:T(8,128)}, f32[2,4,48,128]{3,2,1,0:T(8,128)S(1)}, u32[]{:S(2)}, u32[]{:S(2)}) collective-permute-start(f32[2,4,48,128]{3,2,1,0:T(8,128)} %get-tuple-element.27), channel_id=1, source_target_pairs={{0,1},{1,0},{2,3},{3,2},{4,5},{5,4},{6,7},{7,6},{8,9},{9,8},{10,11... | collective-permute-start | bytes 589832 | tf_op jit(solution)/shard_map/share_near/ppermute | solution.py:371
  4.8 2.0 %collective-permute-start.1 = (f32[2,4,48,128]{3,2,1,0:T(8,128)}, f32[2,4,48,128]{3,2,1,0:T(8,128)S(1)}, u32[]{:S(2)}, u32[]{:S(2)}) collective-permute-start(f32[2,4,48,128]{3,2,1,0:T(8,128)} %get-tuple-element.28), channel_id=1, source_target_pairs={{1,2},{3,4},{5,6},{2,1},{4,3},{6,5},{9,10},{11,12},{13,14},{10,9},... | collective-permute-start | bytes 589832 | tf_op jit(solution)/shard_map/share_far/ppermute | solution.py:371
  6.8 2.7 %collective-permute-done.share_near = f32[2,4,48,128]{3,2,1,0:T(8,128)S(1)} collective-permute-done((f32[2,4,48,128]{3,2,1,0:T(8,128)}, f32[2,4,48,128]{3,2,1,0:T(8,128)S(1)}, u32[]{:S(2)}, u32[]{:S(2)}) %collective-permute-start) | collective-permute-done | bytes 196640 | tf_op jit(solution)/shard_map/share_near/ppermute | solution.py:371
  9.6 3.8 %collective-permute-done.1.share_far = f32[2,4,48,128]{3,2,1,0:T(8,128)S(1)} collective-permute-done((f32[2,4,48,128]{3,2,1,0:T(8,128)}, f32[2,4,48,128]{3,2,1,0:T(8,128)S(1)}, u32[]{:S(2)}, u32[]{:S(2)}) %collective-permute-start.1) | collective-permute-done | bytes 196640 | tf_op jit(solution)/shard_map/share_far/ppermute | solution.py:371
  13.4 2.1 %collective-permute-start.2 = (f32[2,2,4,48,128]{4,3,2,1,0:T(8,128)S(1)}, f32[2,2,4,48,128]{4,3,2,1,0:T(8,128)S(1)}, u32[]{:S(2)}, u32[]{:S(2)}) collective-permute-start(f32[2,2,4,48,128]{4,3,2,1,0:T(8,128)S(1)} %pad_maximum_fusion), channel_id=1, source_target_pairs={{0,8},{8,0},{16,24},{24,16},{1,9},{9,1},{17,25},{25,17},{2,10},{10... | collective-permute-start | bytes 1179656 | tf_op jit(solution)/shard_map/mates/ppermute | solution.py:371
  15.4 0.0 collective-permute-start.3
  15.4 3.3 %collective-permute-start.4 = (f32[2,4,32,128]{3,2,1,0:T(8,128)}, f32[2,4,32,128]{3,2,1,0:T(8,128)S(1)}, u32[]{:S(2)}, u32[]{:S(2)}) collective-permute-start(f32[2,4,32,128]{3,2,1,0:T(8,128)} %get-tuple-element.31), channel_id=1, source_target_pairs={{1,2},{3,4},{5,6},{2,1},{4,3},{6,5},{9,10},{11,12},{13,14},{10,9},... | collective-permute-start | bytes 393224 | tf_op jit(solution)/shard_map/late_far/ppermute | solution.py:371
  18.7 0.1 collective-permute-start.8
  18.8 3.2 %collective-permute-start.9 = (f32[2,4,32,128]{3,2,1,0:T(8,128)}, f32[2,4,32,128]{3,2,1,0:T(8,128)S(1)}, u32[]{:S(2)}, u32[]{:S(2)}) collective-permute-start(f32[2,4,32,128]{3,2,1,0:T(8,128)} %get-tuple-element.39), channel_id=1, source_target_pairs={{1,2},{3,4},{5,6},{2,1},{4,3},{6,5},{9,10},{11,12},{13,14},{10,9},... | collective-permute-start | bytes 393224 | tf_op jit(solution)/shard_map/early_far/ppermute | solution.py:371
  22.0 0.0 collective-permute-done.3.near
  22.0 1.5 %collective-permute-done.4.far = f32[2,4,32,128]{3,2,1,0:T(8,128)S(1)} collective-permute-done((f32[2,4,32,128]{3,2,1,0:T(8,128)}, f32[2,4,32,128]{3,2,1,0:T(8,128)S(1)}, u32[]{:S(2)}, u32[]{:S(2)}) %collective-permute-start.4) | collective-permute-done | bytes 131104 | tf_op jit(solution)/shard_map/late_far/ppermute | solution.py:371
  23.5 0.0 collective-permute-done.2.mates
  23.5 0.0 copy-start
  23.5 1.0 %copy-done = f32[4,4,64,128]{3,2,1,0:T(8,128)S(1)} copy-done((f32[4,4,64,128]{3,2,1,0:T(8,128)S(1)}, f32[4,4,64,128]{3,2,1,0:T(8,128)}, u32[]{:S(2)}) %copy-start) | copy-done | bytes 524312
  24.6 0.0 copy-start.2
  24.6 0.9 %copy-done.2 = f32[2,4,64,128]{3,2,1,0:T(8,128)S(1)} copy-done((f32[2,4,64,128]{3,2,1,0:T(8,128)S(1)}, f32[2,4,64,128]{3,2,1,0:T(8,128)}, u32[]{:S(2)}) %copy-start.2) | copy-done | bytes 262168
  25.5 0.0 copy-start.1
  25.5 5.4 %late_first_sweep.1 = (f32[6,4,176,128]{3,2,1,0:T(8,128)S(1)}, f32[3,4,128,128]{3,2,1,0:T(8,128)S(1)}, f32[2,4,64,128]{3,2,1,0:T(8,128)S(1)}, f32[2,4,48,128]{3,2,1,0:T(8,128)S(1)}, f32[2,4,48,128]{3,2,1,0:T(8,128)S(1)}) custom-call(f32[4,4,64,128]{3,2,1,0:T(8,128)S(1)} %copy-done, f32[2,4,48,128]{3,2,1,0:T(8,128)S(1)} %collective-permute-done.share_near, ...), custom_call_target="tpu_custom_call" | custom-call | flops 6000000000 | bytes 1048576 | tf_op jit(solution)/shard_map/late_first_sweep/pallas_call | solution.py:30
  30.9 0.1 collective-permute-start.5
  31.0 4.1 %collective-permute-start.6 = (f32[2,4,48,128]{3,2,1,0:T(8,128)S(1)}, f32[2,4,48,128]{3,2,1,0:T(8,128)S(1)}, u32[]{:S(2)}, u32[]{:S(2)}) collective-permute-start(f32[2,4,48,128]{3,2,1,0:T(8,128)S(1)} %get-tuple-element.36), channel_id=1, source_target_pairs={{1,2},{3,4},{5,6},{2,1},{4,3},{6,5},{9,10},{11,12},{13,14},{10,9},... | collective-permute-start | bytes 589832 | tf_op jit(solution)/shard_map/late_settled_far/ppermute | solution.py:371
  35.1 0.0 collective-permute-done.8.near
  35.1 0.0 collective-permute-done.9.far
  35.1 0.0 copy-done.1
  35.1 5.1 %early_first_sweep.1 = (f32[2,4,64,128]{3,2,1,0:T(8,128)S(1)}, f32[2,4,48,128]{3,2,1,0:T(8,128)S(1)}, f32[2,4,48,128]{3,2,1,0:T(8,128)S(1)}) custom-call(f32[6,4,176,128]{3,2,1,0:T(8,128)S(1)} %get-tuple-element.33.coeffs, f32[2,4,64,128]{3,2,1,0:T(8,128)S(1)} %copy-done.1, f32[2,4,32,128]{3,2,1,0:T(8,128)S(1)} %collective-permute-done.8.near, ...), custom_call_target="tpu_custom_call" | custom-call | flops 6000000000 | bytes 1048576 | tf_op jit(solution)/shard_map/early_first_sweep/pallas_call | solution.py:30
  40.2 0.1 collective-permute-start.10
  40.3 3.2 %collective-permute-start.11 = (f32[2,4,48,128]{3,2,1,0:T(8,128)S(1)}, f32[2,4,48,128]{3,2,1,0:T(8,128)S(1)}, u32[]{:S(2)}, u32[]{:S(2)}) collective-permute-start(f32[2,4,48,128]{3,2,1,0:T(8,128)S(1)} %get-tuple-element.42), channel_id=1, source_target_pairs={{1,2},{3,4},{5,6},{2,1},{4,3},{6,5},{9,10},{11,12},{13,14},{10,9},... | collective-permute-start | bytes 589832 | tf_op jit(solution)/shard_map/early_settled_far/ppermute | solution.py:371
  43.5 0.0 collective-permute-done.5.near
  43.6 0.0 collective-permute-done.6.far
  43.6 7.0 %late_second_sweep.1 = f32[3,4,96,128]{3,2,1,0:T(8,128)S(1)} custom-call(f32[6,4,176,128]{3,2,1,0:T(8,128)S(1)} %get-tuple-element.33.coeffs, f32[2,4,64,128]{3,2,1,0:T(8,128)S(1)} %get-tuple-element.34.own.settled_last, f32[2,4,48,128]{3,2,1,0:T(8,128)S(1)} %collective-permute-done.5.near, f32[2,4,48,128]{3,2,1,0:T(8,128)S(1)} %collective-permute-done.6.far), custom_call_target="tpu_custom_call" | custom-call | flops 6000000000 | bytes 1048576 | tf_op jit(solution)/shard_map/late_second_sweep/pallas_call | solution.py:30
  50.6 3.7 %collective-permute-start.7 = (f32[3,4,96,128]{3,2,1,0:T(8,128)S(1)}, f32[3,4,96,128]{3,2,1,0:T(8,128)S(1)}, u32[]{:S(2)}, u32[]{:S(2)}) collective-permute-start(f32[3,4,96,128]{3,2,1,0:T(8,128)S(1)} %late_second_sweep.1), channel_id=1, source_target_pairs={{0,8},{8,16},{16,24},{24,0},{1,9},{9,17},{17,25},{25,1},{2,10},{10... | collective-permute-start | bytes 1769480 | tf_op jit(solution)/shard_map/next_slab/ppermute | solution.py:371
  54.3 0.0 collective-permute-done.10.near
  54.3 0.0 collective-permute-done.11.far
  54.3 7.0 %early_second_sweep.1 = (f32[2,4,96,128]{3,2,1,0:T(8,128)S(1)}, f32[2,4,96,128]{3,2,1,0:T(8,128)S(1)}) custom-call(f32[6,4,176,128]{3,2,1,0:T(8,128)S(1)} %get-tuple-element.33.coeffs, f32[2,4,64,128]{3,2,1,0:T(8,128)S(1)} %get-tuple-element.40.own, f32[2,4,48,128]{3,2,1,0:T(8,128)S(1)} %collective-permute-done.10.near, ...), custom_call_target="tpu_custom_call" | custom-call | flops 6000000000 | bytes 1048576 | tf_op jit(solution)/shard_map/early_second_sweep/pallas_call | solution.py:30
  61.3 0.0 collective-permute-done.7.arrived
  61.3 1.1 %slab_value.1 = (f32[4,4,64,128]{3,2,1,0:T(8,128)S(1)}, f32[4,64,128]{2,1,0:T(8,128)S(1)}) custom-call(f32[3,4,128,128]{3,2,1,0:T(8,128)S(1)} %get-tuple-element.32.raw, f32[3,4,96,128]{3,2,1,0:T(8,128)S(1)} %collective-permute-done.7.arrived, f32[2,4,96,128]{3,2,1,0:T(8,128)S(1)} %get-tuple-element.43.settled, ...), custom_call_target="tpu_custom_call" | custom-call | bytes 1048576 | tf_op jit(solution)/shard_map/slab_value/pallas_call | solution.py:30
  62.4 1.9 %collective-permute-start.12 = (f32[4,32,128]{2,1,0:T(8,128)S(1)}, f32[4,32,128]{2,1,0:T(8,128)S(1)}, u32[]{:S(2)}, u32[]{:S(2)}) collective-permute-start(f32[4,32,128]{2,1,0:T(8,128)S(1)} %get-tuple-element.47), channel_id=1, source_target_pairs={{0,1},{1,2},{2,3},{3,4},{4,5},{5,6},{6,7},{8,9},{9,10},{10,11},{11... | collective-permute-start | bytes 196616 | tf_op jit(solution)/shard_map/slab_down/ppermute | solution.py:371
  64.4 4.3 %collective-permute-start.13 = (f32[4,32,128]{2,1,0:T(8,128)S(1)}, f32[4,32,128]{2,1,0:T(8,128)S(1)}, u32[]{:S(2)}, u32[]{:S(2)}) collective-permute-start(f32[4,32,128]{2,1,0:T(8,128)S(1)} %get-tuple-element.48), channel_id=1, source_target_pairs={{1,0},{2,1},{3,2},{4,3},{5,4},{6,5},{7,6},{9,8},{10,9},{11,10},{12... | collective-permute-start | bytes 196616 | tf_op jit(solution)/shard_map/slab_up/ppermute | solution.py:371
  68.6 8.8 %all-gather = f32[16,64,128]{2,1,0:T(8,128)S(1)} all-gather(f32[4,64,128]{2,1,0:T(8,128)S(1)} %get-tuple-element.45), channel_id=2, replica_groups=mesh['tm'=4,'space'=8] {'tm'}, dimensions={0}, use_global_device_ids=true | all-gather | bytes 655360 | tf_op jit(solution)/shard_map/all_gather | solution.py:417
  77.4 0.0 collective-permute-done.12
  77.4 0.0 collective-permute-done.13
  77.4 7.3 %all-gather.1 = f32[8,4,32,128]{3,2,1,0:T(8,128)S(1)} all-gather(f32[2,4,32,128]{3,2,1,0:T(8,128)S(1)} %pad_maximum_fusion.1), channel_id=3, replica_groups=mesh['tm'=4,'space'=8] {'tm'}, dimensions={0}, use_global_device_ids=true | all-gather | bytes 655360 | tf_op jit(solution)/shard_map/all_gather | solution.py:418
  84.7 8.0 %close.1 = f32[4,64,512]{2,1,0:T(8,128)} custom-call(f32[3,4,128,128]{3,2,1,0:T(8,128)S(1)} %get-tuple-element.32.raw, f32[4,4,64,128]{3,2,1,0:T(8,128)S(1)} %bitcast.6, f32[4,2,4,32,128]{4,3,2,1,0:T(8,128)S(1)} %bitcast.7, f32[3,4,96,128]{3,2,1,0:T(8,128)S(1)} %collective-permute-done.7.arrived, f32[2,4,96,128]{3,2,1,0:T(8,128)S(1)} %get-tuple-element.43.settled, ...), custom_call_target="tpu_custom_call" | custom-call | bytes 1048576 | tf_op jit(solution)/shard_map/close/pallas_call | solution.py:30
  (3 shorter events, 0.0 us)
Async XLA Ops:
  3.5 6.0 %collective-permute-start = (f32[2,4,48,128]{3,2,1,0:T(8,128)}, f32[2,4,48,128]{3,2,1,0:T(8,128)S(1)}, u32[]{:S(2)}, u32[]{:S(2)}) collective-permute-start(f32[2,4,48,128]{3,2,1,0:T(8,128)} %get-tuple-element.27), channel_id=1, source_target_pairs={{0,1},{1,0},{2,3},{3,2},{4,5},{5,4},{6,7},{7,6},{8,9},{9,8},{10,11... | collective-permute-start | bytes 589832 | tf_op jit(solution)/shard_map/share_near/ppermute | solution.py:371
  4.8 8.5 %collective-permute-start.1 = (f32[2,4,48,128]{3,2,1,0:T(8,128)}, f32[2,4,48,128]{3,2,1,0:T(8,128)S(1)}, u32[]{:S(2)}, u32[]{:S(2)}) collective-permute-start(f32[2,4,48,128]{3,2,1,0:T(8,128)} %get-tuple-element.28), channel_id=1, source_target_pairs={{1,2},{3,4},{5,6},{2,1},{4,3},{6,5},{9,10},{11,12},{13,14},{10,9},... | collective-permute-start | bytes 589832 | tf_op jit(solution)/shard_map/share_far/ppermute | solution.py:371
  13.4 10.2 %collective-permute-start.2 = (f32[2,2,4,48,128]{4,3,2,1,0:T(8,128)S(1)}, f32[2,2,4,48,128]{4,3,2,1,0:T(8,128)S(1)}, u32[]{:S(2)}, u32[]{:S(2)}) collective-permute-start(f32[2,2,4,48,128]{4,3,2,1,0:T(8,128)S(1)} %pad_maximum_fusion), channel_id=1, source_target_pairs={{0,8},{8,0},{16,24},{24,16},{1,9},{9,1},{17,25},{25,17},{2,10},{10... | collective-permute-start | bytes 1179656 | tf_op jit(solution)/shard_map/mates/ppermute | solution.py:371
  15.4 6.6 %collective-permute-start.3 = (f32[2,4,32,128]{3,2,1,0:T(8,128)}, f32[2,4,32,128]{3,2,1,0:T(8,128)S(1)}, u32[]{:S(2)}, u32[]{:S(2)}) collective-permute-start(f32[2,4,32,128]{3,2,1,0:T(8,128)} %get-tuple-element.30), channel_id=1, source_target_pairs={{0,1},{1,0},{2,3},{3,2},{4,5},{5,4},{6,7},{7,6},{8,9},{9,8},{10,11... | collective-permute-start | bytes 393224 | tf_op jit(solution)/shard_map/late_near/ppermute | solution.py:371
  15.4 8.1 %collective-permute-start.4 = (f32[2,4,32,128]{3,2,1,0:T(8,128)}, f32[2,4,32,128]{3,2,1,0:T(8,128)S(1)}, u32[]{:S(2)}, u32[]{:S(2)}) collective-permute-start(f32[2,4,32,128]{3,2,1,0:T(8,128)} %get-tuple-element.31), channel_id=1, source_target_pairs={{1,2},{3,4},{5,6},{2,1},{4,3},{6,5},{9,10},{11,12},{13,14},{10,9},... | collective-permute-start | bytes 393224 | tf_op jit(solution)/shard_map/late_far/ppermute | solution.py:371
  18.7 16.4 %collective-permute-start.8 = (f32[2,4,32,128]{3,2,1,0:T(8,128)}, f32[2,4,32,128]{3,2,1,0:T(8,128)S(1)}, u32[]{:S(2)}, u32[]{:S(2)}) collective-permute-start(f32[2,4,32,128]{3,2,1,0:T(8,128)} %get-tuple-element.38), channel_id=1, source_target_pairs={{0,1},{1,0},{2,3},{3,2},{4,5},{5,4},{6,7},{7,6},{8,9},{9,8},{10,11... | collective-permute-start | bytes 393224 | tf_op jit(solution)/shard_map/early_near/ppermute | solution.py:371
  18.8 16.4 %collective-permute-start.9 = (f32[2,4,32,128]{3,2,1,0:T(8,128)}, f32[2,4,32,128]{3,2,1,0:T(8,128)S(1)}, u32[]{:S(2)}, u32[]{:S(2)}) collective-permute-start(f32[2,4,32,128]{3,2,1,0:T(8,128)} %get-tuple-element.39), channel_id=1, source_target_pairs={{1,2},{3,4},{5,6},{2,1},{4,3},{6,5},{9,10},{11,12},{13,14},{10,9},... | collective-permute-start | bytes 393224 | tf_op jit(solution)/shard_map/early_far/ppermute | solution.py:371
  23.5 1.0 %copy-start = (f32[4,4,64,128]{3,2,1,0:T(8,128)S(1)}, f32[4,4,64,128]{3,2,1,0:T(8,128)}, u32[]{:S(2)}) copy-start(f32[4,4,64,128]{3,2,1,0:T(8,128)} %get-tuple-element.26.mine) | copy-start | bytes 1572868
  24.6 0.9 %copy-start.2 = (f32[2,4,64,128]{3,2,1,0:T(8,128)S(1)}, f32[2,4,64,128]{3,2,1,0:T(8,128)}, u32[]{:S(2)}) copy-start(f32[2,4,64,128]{3,2,1,0:T(8,128)} %get-tuple-element.29.own) | copy-start | bytes 786436
  25.5 9.6 %copy-start.1 = (f32[2,4,64,128]{3,2,1,0:T(8,128)S(1)}, f32[2,4,64,128]{3,2,1,0:T(8,128)}, u32[]{:S(2)}) copy-start(f32[2,4,64,128]{3,2,1,0:T(8,128)} %get-tuple-element.37.own) | copy-start | bytes 786436
  30.9 12.7 %collective-permute-start.5 = (f32[2,4,48,128]{3,2,1,0:T(8,128)S(1)}, f32[2,4,48,128]{3,2,1,0:T(8,128)S(1)}, u32[]{:S(2)}, u32[]{:S(2)}) collective-permute-start(f32[2,4,48,128]{3,2,1,0:T(8,128)S(1)} %get-tuple-element.35), channel_id=1, source_target_pairs={{0,1},{1,0},{2,3},{3,2},{4,5},{5,4},{6,7},{7,6},{8,9},{9,8},{10,11... | collective-permute-start | bytes 589832 | tf_op jit(solution)/shard_map/late_settled_near/ppermute | solution.py:371
  31.0 12.6 %collective-permute-start.6 = (f32[2,4,48,128]{3,2,1,0:T(8,128)S(1)}, f32[2,4,48,128]{3,2,1,0:T(8,128)S(1)}, u32[]{:S(2)}, u32[]{:S(2)}) collective-permute-start(f32[2,4,48,128]{3,2,1,0:T(8,128)S(1)} %get-tuple-element.36), channel_id=1, source_target_pairs={{1,2},{3,4},{5,6},{2,1},{4,3},{6,5},{9,10},{11,12},{13,14},{10,9},... | collective-permute-start | bytes 589832 | tf_op jit(solution)/shard_map/late_settled_far/ppermute | solution.py:371
  40.2 14.1 %collective-permute-start.10 = (f32[2,4,48,128]{3,2,1,0:T(8,128)S(1)}, f32[2,4,48,128]{3,2,1,0:T(8,128)S(1)}, u32[]{:S(2)}, u32[]{:S(2)}) collective-permute-start(f32[2,4,48,128]{3,2,1,0:T(8,128)S(1)} %get-tuple-element.41), channel_id=1, source_target_pairs={{0,1},{1,0},{2,3},{3,2},{4,5},{5,4},{6,7},{7,6},{8,9},{9,8},{10,11... | collective-permute-start | bytes 589832 | tf_op jit(solution)/shard_map/early_settled_near/ppermute | solution.py:371
  40.3 14.0 %collective-permute-start.11 = (f32[2,4,48,128]{3,2,1,0:T(8,128)S(1)}, f32[2,4,48,128]{3,2,1,0:T(8,128)S(1)}, u32[]{:S(2)}, u32[]{:S(2)}) collective-permute-start(f32[2,4,48,128]{3,2,1,0:T(8,128)S(1)} %get-tuple-element.42), channel_id=1, source_target_pairs={{1,2},{3,4},{5,6},{2,1},{4,3},{6,5},{9,10},{11,12},{13,14},{10,9},... | collective-permute-start | bytes 589832 | tf_op jit(solution)/shard_map/early_settled_far/ppermute | solution.py:371
  50.6 10.7 %collective-permute-start.7 = (f32[3,4,96,128]{3,2,1,0:T(8,128)S(1)}, f32[3,4,96,128]{3,2,1,0:T(8,128)S(1)}, u32[]{:S(2)}, u32[]{:S(2)}) collective-permute-start(f32[3,4,96,128]{3,2,1,0:T(8,128)S(1)} %late_second_sweep.1), channel_id=1, source_target_pairs={{0,8},{8,16},{16,24},{24,0},{1,9},{9,17},{17,25},{25,1},{2,10},{10... | collective-permute-start | bytes 1769480 | tf_op jit(solution)/shard_map/next_slab/ppermute | solution.py:371
  62.4 15.0 %collective-permute-start.12 = (f32[4,32,128]{2,1,0:T(8,128)S(1)}, f32[4,32,128]{2,1,0:T(8,128)S(1)}, u32[]{:S(2)}, u32[]{:S(2)}) collective-permute-start(f32[4,32,128]{2,1,0:T(8,128)S(1)} %get-tuple-element.47), channel_id=1, source_target_pairs={{0,1},{1,2},{2,3},{3,4},{4,5},{5,6},{6,7},{8,9},{9,10},{10,11},{11... | collective-permute-start | bytes 196616 | tf_op jit(solution)/shard_map/slab_down/ppermute | solution.py:371
  64.4 13.0 %collective-permute-start.13 = (f32[4,32,128]{2,1,0:T(8,128)S(1)}, f32[4,32,128]{2,1,0:T(8,128)S(1)}, u32[]{:S(2)}, u32[]{:S(2)}) collective-permute-start(f32[4,32,128]{2,1,0:T(8,128)S(1)} %get-tuple-element.48), channel_id=1, source_target_pairs={{1,0},{2,1},{3,2},{4,3},{5,4},{6,5},{7,6},{9,8},{10,9},{11,10},{12... | collective-permute-start | bytes 196616 | tf_op jit(solution)/shard_map/slab_up/ppermute | solution.py:371

commit v2 on v1

--- a/solution.py
+++ b/solution.py
@@ -14,6 +14,7 @@
 PAD = 8
 NEAR = 16
 FINE = SUBSTEPS * COARSEN_ONE
+ALONE = 61 * 2**20
 VMEM_LIMIT = 24 * 2**20
 
 
@@ -125,43 +126,41 @@
         far[k] = source[k, :, pl.ds(high, width), :]
 
 
-def arrange_kernel(
-    start, guessed, rate, along, across, drive,
-    coeffs, late, early, share_near, share_far, late_near, late_far, early_near, early_far,
-    landed, arrivals, *parts,
-):
-    points, rows, columns = guessed.shape
+def arrange(sources, homes, landed, arrivals, parts):
+    rows, columns = landed.shape[1:]
     blocks = columns // LANES
-    closing = is_last_slab()
-    sources = [rate, along, across, drive] + [guessed.at[k] for k in range(points - 1)]
-    copies = [
-        pltpu.make_async_copy(source, landed.at[k], arrivals.at[k]) for k, source in enumerate(sources)
-    ]
-    final = [
-        pltpu.make_async_copy(source, landed.at[7], arrivals.at[7]) for source in (start, guessed.at[points - 1])
-    ]
-    for copy in copies:
-        copy.start()
-
-    @pl.when(closing)
-    def _():
-        final[0].start()
-
-    @pl.when(jnp.logical_not(closing))
-    def _():
-        final[1].start()
-
+    copies = []
+    for k, choices in enumerate(sources):
+        made = [pltpu.make_async_copy(source, landed.at[k], arrivals.at[k]) for source in choices]
+        copies.append(made[-1])
+        if len(made) == 1:
+            made[0].start()
+        else:
+            pl.when(is_last_slab())(made[0].start)
+            pl.when(jnp.logical_not(is_last_slab()))(made[1].start)
     order = column_order(columns, False)
-    for index, copy in enumerate(copies + final[1:]):
+    for index, copy in enumerate(copies):
         copy.wait()
         for part, value in zip(parts, split_three(landed[index])):
             part[pl.ds(index * rows, rows), :] = value
     result = reorder(parts, order)
-    homes = [coeffs.at[k] for k in range(4)] + [early.at[0], early.at[1], late.at[0], late.at[1]]
     for index, home in enumerate(homes):
         for j in range(blocks):
             home[j] = result[index * rows : (index + 1) * rows, j * LANES : (j + 1) * LANES]
+
+
+def coeffs_kernel(rate, along, across, drive, coeffs, share_near, share_far, landed, arrivals, *parts):
+    sources = [[rate], [along], [across], [drive]]
+    arrange(sources, [coeffs.at[k] for k in range(4)], landed, arrivals, parts)
     sides(coeffs.at[pl.ds(2 * (lax.axis_index("tm") % 2), 2)], share_near, share_far)
+
+
+def points_kernel(
+    start, guessed, late, early, late_near, late_far, early_near, early_far, landed, arrivals, *parts
+):
+    sources = [[guessed.at[0]], [guessed.at[1]], [guessed.at[2]], [start, guessed.at[3]]]
+    homes = [early.at[0], early.at[1], late.at[0], late.at[1]]
+    arrange(sources, homes, landed, arrivals, parts)
     sides(late, late_near, late_far)
     sides(early, early_near, early_far)
 
@@ -190,6 +189,15 @@
             return carry
 
         lax.fori_loop(0, 2, pairs, 0)
+
+
+def window_kernel(own, near, far, a):
+    a[...] = jnp.zeros(a.shape, jnp.float32)
+    rows = own.shape[2]
+    base = (a.shape[2] - rows) // 2 - near.shape[2]
+    for p in range(own.shape[0]):
+        a[p, :, pl.ds(base + near.shape[2], rows), :] = own[p]
+    fill(a, base, own, near, far, range(own.shape[0]))
 
 
 def load_points(a, b, own, near, far):
@@ -215,7 +223,7 @@
 
 
 def open_kernel(
-    mine, share_near, share_far, mates, own, near, far,
+    mine, share_near, share_far, mates, loaded,
     coeffs, raw_out, settled, next_near, next_far, raw, a, b,
 ):
     rows = mine.shape[2]
@@ -229,7 +237,11 @@
     clear_ends(coeffs)
     raw_rows = raw_out.shape[2]
     raw_out[...] = raw[0:3, :, pl.ds((total - raw_rows) // 2, raw_rows), :]
-    first_sweep(coeffs, own, near, far, settled, next_near, next_far, a, b)
+    a[...] = loaded[...]
+    b[...] = loaded[...]
+    run_sweep(a, b, coeffs, PAD + NEAR, rows + 2 * FINE, a.shape[0])
+    settled[...] = a[:, :, pl.ds(PAD + NEAR + FINE, rows), :]
+    sides(settled, next_near, next_far)
 
 
 def second_sweep(coeffs, own, near, far, a, b):
@@ -238,19 +250,29 @@
     return base, total, keep
 
 
+def moved(packed, rows):
+    ends = (rows + 2 * NEAR, 2 * rows + 3 * NEAR, 3 * rows + 3 * NEAR)
+    starts = (0,) + ends[:2]
+    return [packed.at[:, pl.ds(start, end - start), :] for start, end in zip(starts, ends)]
+
+
 def late_kernel(coeffs, own, near, far, shift_out, a, b):
     base, total, keep = second_sweep(coeffs, own, near, far, a, b)
-    shift_out[2] = a[1, :, keep, :]
+    rows = own.shape[2]
+    residual, swept, settled = moved(shift_out, rows)
+    settled[...] = own[1]
+    before = a[1, :, keep, :]
+    residual[...] = before
     run_sweep(a, b, coeffs, base, total, own.shape[0])
-    shift_out[1] = a[1, :, keep, :]
+    swept[...] = a[1, :, pl.ds(base + FINE + NEAR // 2, rows + NEAR), :]
 
     @pl.when(is_last_slab())
     def _():
-        shift_out[0] = shift_out[2] - shift_out[2]
+        residual[...] = residual[...] - residual[...]
 
     @pl.when(jnp.logical_not(is_last_slab()))
     def _():
-        shift_out[0] = a[0, :, keep, :] - shift_out[2]
+        residual[...] = a[0, :, keep, :] - residual[...]
 
 
 def early_kernel(coeffs, own, near, far, settled_out, swept_out, a, b):
@@ -260,13 +282,15 @@
     swept_out[...] = a[:, :, keep, :]
 
 
-def coarse_step(a, b, coeffs, low, high, points):
-    for _ in range(SUBSTEPS // 2):
-        substep(a, b, coeffs, low, high, points, False)
-        substep(b, a, coeffs, low, high, points, False)
-
-
-def slab_kernel(raw, arrived, settled, swept, settled_last, e_out, c_out, coeffs, a, b):
+def coarse_step(a, b, coeffs, reach, rows, points):
+    own = (a.shape[2] - rows) // 2
+    for step in range(SUBSTEPS):
+        source, target = (a, b) if step % 2 == 0 else (b, a)
+        halo = 8 * -(-(reach - step - 1) // 8)
+        substep(source, target, coeffs, own - halo, own + rows + halo, points, False)
+
+
+def slab_kernel(raw, arrived, settled, swept, settled_last, e_out, c_out, c_near, c_far, coeffs, a, b):
     kept = settled.shape[2]
     rows = settled_last.shape[2]
     weights(raw, (raw.shape[2] - kept) // 2, coeffs, kept, float(COARSEN_ONE), False)
@@ -275,22 +299,26 @@
     inner = pl.ds(PAD, kept)
     own = pl.ds(NEAR, rows)
     held = pl.ds(PAD + NEAR, rows)
-    a[0, :, inner, :] = arrived[0]
+    first, second, _ = moved(arrived, rows)
+    trimmed = pl.ds(PAD + NEAR // 2, rows + NEAR)
+    a[0, :, inner, :] = first[...]
     e_out[0] = a[0, :, held, :]
     for position in range(1, COARSEN_TWO):
-        trim = 8 * ((position - 1) * SUBSTEPS // 8)
-        coarse_step(a, b, coeffs, PAD + trim, PAD + kept - trim, 1)
+        coarse_step(a, b, coeffs, SUBSTEPS * (COARSEN_TWO - position), rows, 1)
         if position == 1:
-            a[0, :, inner, :] = a[0, :, inner, :] + (arrived[1] - settled[0])
+            value = second[...] - settled[0, :, pl.ds(NEAR // 2, rows + NEAR), :]
+            a[0, :, trimmed, :] = a[0, :, trimmed, :] + value
         elif position == 2:
             a[0, :, inner, :] = a[0, :, inner, :] + (swept[0] - settled[1])
         else:
             a[0, :, held, :] = a[0, :, held, :] + (swept[1, :, own, :] - settled_last[0])
         e_out[position] = a[0, :, held, :]
-    c_out[...] = e_out[COARSEN_TWO - 1]
+    c_out[0] = e_out[COARSEN_TWO - 1]
+    sides(c_out, c_near, c_far)
 
 
 def close_kernel(raw, gathered, edges, arrived, settled, settled_last, e, out, level_coeffs, top_coeffs, a, b, w, l, x, y, *parts):
+    even = lax.axis_index("space") % 2 == 0
     slabs = gathered.shape[0]
     chain = slabs - 1
     rows = gathered.shape[2]
@@ -302,25 +330,26 @@
     for ref in (a, b, x, y):
         clear_ends(ref)
     for k in range(chain):
-        a[k, :, pl.ds(PAD, reach), :] = edges[k, 0]
         a[k, :, pl.ds(PAD + reach, rows), :] = gathered[k]
-        a[k, :, pl.ds(PAD + reach + rows, reach), :] = edges[k, 1]
+        low, high = PAD, PAD + reach + rows
+        partner = pl.multiple_of(jnp.where(even, high, low), 8)
+        other = pl.multiple_of(jnp.where(even, low, high), 8)
+        a[k, :, pl.ds(partner, reach), :] = edges[k, 0]
+        a[k, :, pl.ds(other, reach), :] = edges[k, 1]
     inner = pl.ds(PAD, total)
     w[0] = jnp.zeros(w.shape[1:], jnp.float32)
     l[0] = jnp.zeros(l.shape[1:], jnp.float32)
     for k in range(chain):
         w[k + 1] = a[k, :, inner, :]
     for step in range(COARSEN_TWO):
-        trim = 8 * (step * SUBSTEPS // 8)
-        coarse_step(a, b, level_coeffs, PAD + trim, PAD + total - trim, chain)
-    used = COARSEN_TWO * SUBSTEPS
+        coarse_step(a, b, level_coeffs, reach - step * SUBSTEPS, rows, chain)
+    left = reach - COARSEN_TWO * SUBSTEPS
     x[0, :, inner, :] = a[0, :, inner, :]
     l[1] = x[0, :, inner, :]
     for k in range(1, chain):
         w[k + 1] = w[k + 1] + l[k]
-        trim = 8 * (used // 8)
-        coarse_step(x, y, top_coeffs, PAD + trim, PAD + total - trim, 1)
-        used += SUBSTEPS
+        coarse_step(x, y, top_coeffs, left if k < chain - 1 else SUBSTEPS, rows, 1)
+        left -= SUBSTEPS
         x[0, :, inner, :] = x[0, :, inner, :] + a[k, :, inner, :]
         l[k + 1] = x[0, :, inner, :]
     slab = lax.axis_index("tm")
@@ -330,9 +359,11 @@
     blocks = gathered.shape[1]
     for position in range(COARSEN_TWO):
         if position < COARSEN_TWO - 1:
-            trim = 8 * ((reach - COARSEN_TWO * SUBSTEPS + SUBSTEPS * position) // 8)
-            coarse_step(x, y, level_coeffs, PAD + trim, PAD + total - trim, 1)
-            settled_here = (arrived.at[2] if position == 0 else settled.at[position - 1]).at[:, pl.ds(NEAR, rows), :]
+            coarse_step(x, y, level_coeffs, SUBSTEPS * (COARSEN_TWO - 1 - position), rows, 1)
+            if position == 0:
+                settled_here = moved(arrived, rows)[2]
+            else:
+                settled_here = settled.at[position - 1, :, pl.ds(NEAR, rows), :]
             value = x[0, :, held, :]
         else:
             settled_here = settled_last.at[0]
@@ -353,14 +384,17 @@
     strips = lax.axis_size("space")
 
     field = (blocks, rows, LANES)
-    parts = [pltpu.VMEM((8 * rows, columns), jnp.bfloat16)] * 3
-    landing = [pltpu.VMEM((8, rows, columns), jnp.float32), pltpu.SemaphoreType.DMA((8,))]
     wide_field = (blocks, FINE + NEAR, LANES)
     halo = (blocks, FINE, LANES)
-    coeffs, late, early, share_near, share_far, late_near, late_far, early_near, early_far = call(
-        arrange_kernel, "arrange",
-        [(4,) + field, (2,) + field, (2,) + field] + [(2,) + wide_field] * 2 + [(2,) + halo] * 4,
-        landing + parts, start_field, guessed, diffusion, peclet_x, peclet_y, source, far=True, grant=61 * 2**20,
+    landing = [pltpu.VMEM((4, rows, columns), jnp.float32), pltpu.SemaphoreType.DMA((4,))]
+    parts = [pltpu.VMEM((4 * rows, columns), jnp.bfloat16)] * 3
+    coeffs, share_near, share_far = call(
+        coeffs_kernel, "arrange_coeffs", [(4,) + field] + [(2,) + wide_field] * 2,
+        landing + parts, diffusion, peclet_x, peclet_y, source, far=True, grant=ALONE,
+    )
+    late, early, late_near, late_far, early_near, early_far = call(
+        points_kernel, "arrange_points", [(2,) + field] * 2 + [(2,) + halo] * 4,
+        landing + parts, start_field, guessed, cost=2 * 10**9, far=True,
     )
     swap = [(i, i ^ 1) for i in range(strips)]
     cross = [(i, i + 1) for i in range(1, strips - 1, 2)] + [(i + 1, i) for i in range(1, strips - 1, 2)]
@@ -376,6 +410,7 @@
     share_sides = exchange("share", share_near, share_far)
     late_sides = exchange("late", late_near, late_far)
     mates = send("mates", jnp.stack(share_sides), "tm", mate)
+    early_near, early_far, _ = lax.optimization_barrier((early_near, early_far, share_sides[0]))
     early_sides = exchange("early", early_near, early_far)
 
     reach = 8 * -(-(SUBSTEPS * (2 * COARSEN_TWO - 1 + max(slabs - 3, 0))) // 8)
@@ -386,11 +421,12 @@
     work = 6 * 10**9
     near = (2, blocks, rows + 2 * NEAR, LANES)
     sent = [(2,) + field] + [(2,) + wide_field] * 2
+    (loaded,) = call(window_kernel, "late_window", [(2,) + window], [], late, *late_sides, cost=10 * 10**9)
     fine, raw, late_settled, late_near, late_far = call(
         open_kernel, "late_first_sweep",
         [(6,) + window, (3, blocks, rows + 2 * spread, LANES)] + sent,
         [pltpu.VMEM((4, blocks, total, LANES), jnp.float32)] + pair,
-        coeffs, *share_sides, mates, late, *late_sides, cost=work,
+        coeffs, *share_sides, mates, loaded, cost=10**9,
     )
     late_sides = exchange("late_settled", late_near, late_far)
     early_settled, early_near, early_far = call(
@@ -398,24 +434,21 @@
     )
     early_sides = exchange("early_settled", early_near, early_far)
     (outgoing,) = call(
-        late_kernel, "late_second_sweep", [(3,) + near[1:]], pair, fine, late_settled, *late_sides, cost=work
+        late_kernel, "late_second_sweep", [(blocks, 3 * (rows + NEAR), LANES)], pair, fine, late_settled, *late_sides, cost=work
     )
     arrived = send("next_slab", outgoing, "tm", [(i, (i + 1) % slabs) for i in range(slabs)])
     settled, swept = call(
         early_kernel, "early_second_sweep", [near, near], pair, fine, early_settled, *early_sides, cost=work
     )
     padded = (blocks, rows + 2 * NEAR + 2 * PAD, LANES)
-    e, c_value = call(
-        slab_kernel, "slab_value", [(COARSEN_TWO,) + field, field],
+    e, c_value, c_near, c_far = call(
+        slab_kernel, "slab_value", [(COARSEN_TWO,) + field, (1,) + field] + [(1, blocks, reach, LANES)] * 2,
         [pltpu.VMEM((5,) + padded, jnp.float32)] + [pltpu.VMEM((1,) + padded, jnp.float32)] * 2,
         raw, arrived, settled, swept, late_settled,
     )
-    forward = [(i, i + 1) for i in range(strips - 1)]
-    backward = [(i + 1, i) for i in range(strips - 1)]
-    from_above = send("slab_down", c_value[:, rows - reach :, :], "space", forward)
-    from_below = send("slab_up", c_value[:, :reach, :], "space", backward)
-    gathered = lax.all_gather(c_value, "tm")
-    edges = lax.all_gather(jnp.stack([from_above, from_below]), "tm")
+    c_sides = exchange("slab", c_near, c_far)
+    gathered = lax.all_gather(c_value[0], "tm")
+    edges = lax.all_gather(jnp.concatenate(c_sides), "tm")
 
     span = rows + 2 * reach
     wide = (blocks, span + 2 * PAD, LANES)

time: 93.5 us -> 84.5 us (0.904)
  waiting for transfers between devices: 8.01 us -> 0.94 us
  starting transfers between devices: 29.4 us -> 26.6 us
  blocking collectives: 16.1 us -> 15 us
    ppermute x14, waiting for transfers between devices: 8.01 us -> 0.94 us  [send(): return lax.ppermute(value, axis, route)]
    ppermute x14, starting transfers between devices: 29.4 us -> 26.6 us  [send(): return lax.ppermute(value, axis, route)]
    all_gather x2, blocking collectives: 16.1 us -> 15 us  [the longest x1 7.68 us: on_device(): gathered = lax.all_gather(c_value[0], 'tm')]
    pallas_call x7 -> x9, Pallas kernels: 37 us -> 37.8 us  [call(): pl.pallas_call(kernel, out_shape=[jax.ShapeDtypeStruct(shape, jnp.float32...]
  transfers between devices with their start and end apart: 14 -> 14, of which waited for: 3 -> 1; matrix products, arithmetic and copies ran while one was open for 0% -> 0% of each run, Pallas kernels for 26% -> 31%
where the time goes in v2:
time: 84.5 us; the launch traced here: 83.5 us
  Pallas kernels  37.8 us (45%)
  starting transfers between devices  26.6 us (31%)
  blocking collectives  15 us (18%)
  local copies, waits for them, and re-layouts  2.9 us (3%)
  waiting for transfers between devices  0.94 us (1%)
    pallas_call x9, Pallas kernels, call(): pl.pallas_call(kernel, out_shape=[jax.ShapeDtypeStruct(shape, jnp.float32...  37.8 us
    ppermute x14, starting transfers between devices, send(): return lax.ppermute(value, axis, route)  26.6 us
    all_gather x1, blocking collectives, on_device(): gathered = lax.all_gather(c_value[0], 'tm')  7.68 us
    all_gather x1, blocking collectives, on_device(): edges = lax.all_gather(jnp.concatenate(c_sides), 'tm')  7.29 us
    unnamed x6, local copies, waits for them, and re-layouts  2.9 us
  transfers between devices with their start and end apart: 14, of which 1 were waited for; matrix products, arithmetic and copies ran while one was open for 0% of the time, Pallas kernels for 31%

profile of v2, /device:TPU:25, one launch (start us, length us, event | category | flops | bytes accessed | tf_op | source)
XLA Modules:
  0.0 83.5 jit_solution(17826942758755354555)
XLA Ops:
  0.0 2.6 %arrange_coeffs.1 = (f32[4,4,64,128]{3,2,1,0:T(8,128)}, f32[2,4,48,128]{3,2,1,0:T(8,128)}, f32[2,4,48,128]{3,2,1,0:T(8,128)}) custom-call(f32[64,512]{1,0:T(8,128)} %rate.1, f32[64,512]{1,0:T(8,128)} %along.1, f32[64,512]{1,0:T(8,128)} %across.1, f32[64,512]{1,0:T(8,128)} %drive.1), custom_call_target="tpu_custom_call" | custom-call | bytes 1048576 | tf_op jit(solution)/shard_map/arrange_coeffs/pallas_call | solution.py:31
  2.6 1.3 %collective-permute-start = (f32[2,4,48,128]{3,2,1,0:T(8,128)}, f32[2,4,48,128]{3,2,1,0:T(8,128)S(1)}, u32[]{:S(2)}, u32[]{:S(2)}) collective-permute-start(f32[2,4,48,128]{3,2,1,0:T(8,128)} %get-tuple-element.31), channel_id=1, source_target_pairs={{0,1},{1,0},{2,3},{3,2},{4,5},{5,4},{6,7},{7,6},{8,9},{9,8},{10,11... | collective-permute-start | bytes 589832 | tf_op jit(solution)/shard_map/share_near/ppermute | solution.py:405
  3.9 2.0 %collective-permute-start.1 = (f32[2,4,48,128]{3,2,1,0:T(8,128)}, f32[2,4,48,128]{3,2,1,0:T(8,128)S(1)}, u32[]{:S(2)}, u32[]{:S(2)}) collective-permute-start(f32[2,4,48,128]{3,2,1,0:T(8,128)} %get-tuple-element.32), channel_id=1, source_target_pairs={{1,2},{3,4},{5,6},{2,1},{4,3},{6,5},{9,10},{11,12},{13,14},{10,9},... | collective-permute-start | bytes 589832 | tf_op jit(solution)/shard_map/share_far/ppermute | solution.py:405
  5.9 0.0 copy-start
  5.9 1.0 %copy-done = f32[4,64,512]{2,1,0:T(8,128)S(1)} copy-done((f32[4,64,512]{2,1,0:T(8,128)S(1)}, f32[4,64,512]{2,1,0:T(8,128)}, u32[]{:S(2)}) %copy-start) | copy-done | bytes 524312
  7.0 0.0 copy-start.2
  7.0 0.9 %copy-done.2 = f32[64,512]{1,0:T(8,128)S(1)} copy-done((f32[64,512]{1,0:T(8,128)S(1)}, f32[64,512]{1,0:T(8,128)}, u32[]{:S(2)}) %copy-start.2) | copy-done | bytes 131096
  7.9 1.5 %arrange_points.1 = (f32[2,4,64,128]{3,2,1,0:T(8,128)S(1)}, f32[2,4,64,128]{3,2,1,0:T(8,128)S(1)}, f32[2,4,32,128]{3,2,1,0:T(8,128)S(1)}, f32[2,4,32,128]{3,2,1,...) custom-call(f32[64,512]{1,0:T(8,128)S(1)} %copy-done.2, f32[4,64,512]{2,1,0:T(8,128)S(1)} %copy-done), custom_call_target="tpu_custom_call" | custom-call | flops 2000000000 | bytes 1048576 | tf_op jit(solution)/shard_map/arrange_points/pallas_call | solution.py:31
  9.4 0.1 collective-permute-start.3
  9.5 4.1 %collective-permute-start.4 = (f32[2,4,32,128]{3,2,1,0:T(8,128)S(1)}, f32[2,4,32,128]{3,2,1,0:T(8,128)S(1)}, u32[]{:S(2)}, u32[]{:S(2)}) collective-permute-start(f32[2,4,32,128]{3,2,1,0:T(8,128)S(1)} %get-tuple-element.35), channel_id=1, source_target_pairs={{1,2},{3,4},{5,6},{2,1},{4,3},{6,5},{9,10},{11,12},{13,14},{10,9},... | collective-permute-start | bytes 393224 | tf_op jit(solution)/shard_map/late_far/ppermute | solution.py:405
  13.6 0.0 collective-permute-done.share_near
  13.6 0.0 collective-permute-done.1.share_far
  13.7 1.6 %collective-permute-start.2 = (f32[2,2,4,48,128]{4,3,2,1,0:T(8,128)S(1)}, f32[2,2,4,48,128]{4,3,2,1,0:T(8,128)S(1)}, u32[]{:S(2)}, u32[]{:S(2)}) collective-permute-start(f32[2,2,4,48,128]{4,3,2,1,0:T(8,128)S(1)} %pad_maximum_fusion), channel_id=1, source_target_pairs={{0,8},{8,0},{16,24},{24,16},{1,9},{9,1},{17,25},{25,17},{2,10},{10... | collective-permute-start | bytes 1179656 | tf_op jit(solution)/shard_map/mates/ppermute | solution.py:405
  15.3 0.0 collective-permute-start.8
  15.3 3.4 %collective-permute-start.9 = (f32[2,4,32,128]{3,2,1,0:T(8,128)S(1)}, f32[2,4,32,128]{3,2,1,0:T(8,128)S(1)}, u32[]{:S(2)}, u32[]{:S(2)}) collective-permute-start(f32[2,4,32,128]{3,2,1,0:T(8,128)S(1)} %get-tuple-element.45), channel_id=1, source_target_pairs={{1,2},{3,4},{5,6},{2,1},{4,3},{6,5},{9,10},{11,12},{13,14},{10,9},... | collective-permute-start | bytes 393224 | tf_op jit(solution)/shard_map/early_far/ppermute | solution.py:405
  18.6 0.9 %collective-permute-done.3.near = f32[2,4,32,128]{3,2,1,0:T(8,128)S(1)} collective-permute-done((f32[2,4,32,128]{3,2,1,0:T(8,128)S(1)}, f32[2,4,32,128]{3,2,1,0:T(8,128)S(1)}, u32[]{:S(2)}, u32[]{:S(2)}) %collective-permute-start.3) | collective-permute-done | bytes 131104 | tf_op jit(solution)/shard_map/late_near/ppermute | solution.py:405
  19.6 0.0 collective-permute-done.4.far
  19.6 0.0 copy-start.1
  19.6 0.1 late_window.1.loaded
  19.6 0.0 collective-permute-done.2.mates
  19.6 1.0 %copy-done.1 = f32[4,4,64,128]{3,2,1,0:T(8,128)S(1)} copy-done((f32[4,4,64,128]{3,2,1,0:T(8,128)S(1)}, f32[4,4,64,128]{3,2,1,0:T(8,128)}, u32[]{:S(2)}) %copy-start.1) | copy-done | bytes 524312
  20.6 5.4 %late_first_sweep.1 = (f32[6,4,176,128]{3,2,1,0:T(8,128)S(1)}, f32[3,4,128,128]{3,2,1,0:T(8,128)S(1)}, f32[2,4,64,128]{3,2,1,0:T(8,128)S(1)}, f32[2,4,48,128]{3,2,1,0:T(8,128)S(1)}, f32[2,4,48,128]{3,2,1,0:T(8,128)S(1)}) custom-call(f32[4,4,64,128]{3,2,1,0:T(8,128)S(1)} %copy-done.1, f32[2,4,48,128]{3,2,1,0:T(8,128)S(1)} %collective-permute-done.share_near, ...), custom_call_target="tpu_custom_call" | custom-call | flops 1000000000 | bytes 1048576 | tf_op jit(solution)/shard_map/late_first_sweep/pallas_call | solution.py:31
  26.0 0.1 collective-permute-start.5
  26.1 3.6 %collective-permute-start.6 = (f32[2,4,48,128]{3,2,1,0:T(8,128)S(1)}, f32[2,4,48,128]{3,2,1,0:T(8,128)S(1)}, u32[]{:S(2)}, u32[]{:S(2)}) collective-permute-start(f32[2,4,48,128]{3,2,1,0:T(8,128)S(1)} %get-tuple-element.40), channel_id=1, source_target_pairs={{1,2},{3,4},{5,6},{2,1},{4,3},{6,5},{9,10},{11,12},{13,14},{10,9},... | collective-permute-start | bytes 589832 | tf_op jit(solution)/shard_map/late_settled_far/ppermute | solution.py:405
  29.7 0.0 collective-permute-done.8.near
  29.7 0.0 collective-permute-done.9.far
  29.7 5.1 %early_first_sweep.1 = (f32[2,4,64,128]{3,2,1,0:T(8,128)S(1)}, f32[2,4,48,128]{3,2,1,0:T(8,128)S(1)}, f32[2,4,48,128]{3,2,1,0:T(8,128)S(1)}) custom-call(f32[6,4,176,128]{3,2,1,0:T(8,128)S(1)} %get-tuple-element.37.coeffs, f32[2,4,64,128]{3,2,1,0:T(8,128)S(1)} %get-tuple-element.41.own, f32[2,4,32,128]{3,2,1,0:T(8,128)S(1)} %collective-permute-done.8.near, ...), custom_call_target="tpu_custom_call" | custom-call | flops 6000000000 | bytes 1048576 | tf_op jit(solution)/shard_map/early_first_sweep/pallas_call | solution.py:31
  34.8 0.1 collective-permute-start.10
  34.9 3.4 %collective-permute-start.11 = (f32[2,4,48,128]{3,2,1,0:T(8,128)S(1)}, f32[2,4,48,128]{3,2,1,0:T(8,128)S(1)}, u32[]{:S(2)}, u32[]{:S(2)}) collective-permute-start(f32[2,4,48,128]{3,2,1,0:T(8,128)S(1)} %get-tuple-element.48), channel_id=1, source_target_pairs={{1,2},{3,4},{5,6},{2,1},{4,3},{6,5},{9,10},{11,12},{13,14},{10,9},... | collective-permute-start | bytes 589832 | tf_op jit(solution)/shard_map/early_settled_far/ppermute | solution.py:405
  38.3 0.0 collective-permute-done.5.near
  38.3 0.0 collective-permute-done.6.far
  38.3 7.2 %late_second_sweep.1 = f32[4,240,128]{2,1,0:T(8,128)S(1)} custom-call(f32[6,4,176,128]{3,2,1,0:T(8,128)S(1)} %get-tuple-element.37.coeffs, f32[2,4,64,128]{3,2,1,0:T(8,128)S(1)} %get-tuple-element.38.own.settled_last, f32[2,4,48,128]{3,2,1,0:T(8,128)S(1)} %collective-permute-done.5.near, f32[2,4,48,128]{3,2,1,0:T(8,128)S(1)} %collective-permute-done.6.far), custom_call_target="tpu_custom_call" | custom-call | flops 6000000000 | bytes 1048576 | tf_op jit(solution)/shard_map/late_second_sweep/pallas_call | solution.py:31
  45.5 3.4 %collective-permute-start.7 = (f32[4,240,128]{2,1,0:T(8,128)S(1)}, f32[4,240,128]{2,1,0:T(8,128)S(1)}, u32[]{:S(2)}, u32[]{:S(2)}) collective-permute-start(f32[4,240,128]{2,1,0:T(8,128)S(1)} %late_second_sweep.1), channel_id=1, source_target_pairs={{0,8},{8,16},{16,24},{24,0},{1,9},{9,17},{17,25},{25,1},{2,10},{10... | collective-permute-start | bytes 1474568 | tf_op jit(solution)/shard_map/next_slab/ppermute | solution.py:405
  48.9 0.0 collective-permute-done.10.near
  48.9 0.0 collective-permute-done.11.far
  48.9 7.0 %early_second_sweep.1 = (f32[2,4,96,128]{3,2,1,0:T(8,128)S(1)}, f32[2,4,96,128]{3,2,1,0:T(8,128)S(1)}) custom-call(f32[6,4,176,128]{3,2,1,0:T(8,128)S(1)} %get-tuple-element.37.coeffs, f32[2,4,64,128]{3,2,1,0:T(8,128)S(1)} %get-tuple-element.46.own, f32[2,4,48,128]{3,2,1,0:T(8,128)S(1)} %collective-permute-done.10.near, ...), custom_call_target="tpu_custom_call" | custom-call | flops 6000000000 | bytes 1048576 | tf_op jit(solution)/shard_map/early_second_sweep/pallas_call | solution.py:31
  55.9 0.0 collective-permute-done.7.arrived
  55.9 1.0 %slab_value.1 = (f32[4,4,64,128]{3,2,1,0:T(8,128)S(1)}, f32[1,4,64,128]{3,2,1,0:T(8,128)S(1)}, f32[1,4,32,128]{3,2,1,0:T(8,128)S(1)}, f32[1,4,32,128]{3,2,1,0:T(8,128)S(1)}) custom-call(f32[3,4,128,128]{3,2,1,0:T(8,128)S(1)} %get-tuple-element.36.raw, f32[4,240,128]{2,1,0:T(8,128)S(1)} %collective-permute-done.7.arrived, ...), custom_call_target="tpu_custom_call" | custom-call | bytes 1048576 | tf_op jit(solution)/shard_map/slab_value/pallas_call | solution.py:31
  56.9 0.1 collective-permute-start.12
  57.0 3.5 %collective-permute-start.13 = (f32[1,4,32,128]{3,2,1,0:T(8,128)S(1)}, f32[1,4,32,128]{3,2,1,0:T(8,128)S(1)}, u32[]{:S(2)}, u32[]{:S(2)}) collective-permute-start(f32[1,4,32,128]{3,2,1,0:T(8,128)S(1)} %get-tuple-element.53), channel_id=1, source_target_pairs={{1,2},{3,4},{5,6},{2,1},{4,3},{6,5},{9,10},{11,12},{13,14},{10,9},... | collective-permute-start | bytes 196616 | tf_op jit(solution)/shard_map/slab_far/ppermute | solution.py:405
  60.5 7.7 %all_gather.9.gathered = f32[4,4,64,128]{3,2,1,0:T(8,128)S(1)} all-gather(f32[1,4,64,128]{3,2,1,0:T(8,128)S(1)} %get-tuple-element.51), channel_id=1, replica_groups=mesh['tm'=4,'space'=8] {'tm'}, dimensions={0}, use_global_device_ids=true | all-gather | bytes 655360 | tf_op jit(solution)/shard_map/all_gather | solution.py:450
  68.2 0.0 collective-permute-done.12
  68.2 0.0 collective-permute-done.13
  68.2 7.3 %all-gather = f32[8,4,32,128]{3,2,1,0:T(8,128)S(1)} all-gather(f32[2,4,32,128]{3,2,1,0:T(8,128)S(1)} %pad_maximum_fusion.1), channel_id=2, replica_groups=mesh['tm'=4,'space'=8] {'tm'}, dimensions={0}, use_global_device_ids=true | all-gather | bytes 655360 | tf_op jit(solution)/shard_map/all_gather | solution.py:451
  75.5 7.9 %close.1 = f32[4,64,512]{2,1,0:T(8,128)} custom-call(f32[3,4,128,128]{3,2,1,0:T(8,128)S(1)} %get-tuple-element.36.raw, f32[4,4,64,128]{3,2,1,0:T(8,128)S(1)} %all_gather.9.gathered, f32[4,2,4,32,128]{4,3,2,1,0:T(8,128)S(1)} %bitcast.3, f32[4,240,128]{2,1,0:T(8,128)S(1)} %collective-permute-done.7.arrived, f32[2,4,96,128]{3,2,1,0:T(8,128)S(1)} %get-tuple-element.49.settled, ...), custom_call_target="tpu_custom_call" | custom-call | bytes 1048576 | tf_op jit(solution)/shard_map/close/pallas_call | solution.py:31
  (2 shorter events, 0.0 us)
Async XLA Ops:
  2.6 11.0 %collective-permute-start = (f32[2,4,48,128]{3,2,1,0:T(8,128)}, f32[2,4,48,128]{3,2,1,0:T(8,128)S(1)}, u32[]{:S(2)}, u32[]{:S(2)}) collective-permute-start(f32[2,4,48,128]{3,2,1,0:T(8,128)} %get-tuple-element.31), channel_id=1, source_target_pairs={{0,1},{1,0},{2,3},{3,2},{4,5},{5,4},{6,7},{7,6},{8,9},{9,8},{10,11... | collective-permute-start | bytes 589832 | tf_op jit(solution)/shard_map/share_near/ppermute | solution.py:405
  3.9 9.8 %collective-permute-start.1 = (f32[2,4,48,128]{3,2,1,0:T(8,128)}, f32[2,4,48,128]{3,2,1,0:T(8,128)S(1)}, u32[]{:S(2)}, u32[]{:S(2)}) collective-permute-start(f32[2,4,48,128]{3,2,1,0:T(8,128)} %get-tuple-element.32), channel_id=1, source_target_pairs={{1,2},{3,4},{5,6},{2,1},{4,3},{6,5},{9,10},{11,12},{13,14},{10,9},... | collective-permute-start | bytes 589832 | tf_op jit(solution)/shard_map/share_far/ppermute | solution.py:405
  5.9 1.0 %copy-start = (f32[4,64,512]{2,1,0:T(8,128)S(1)}, f32[4,64,512]{2,1,0:T(8,128)}, u32[]{:S(2)}) copy-start(f32[4,64,512]{2,1,0:T(8,128)} %guessed.1) | copy-start | bytes 1572868
  7.0 0.9 %copy-start.2 = (f32[64,512]{1,0:T(8,128)S(1)}, f32[64,512]{1,0:T(8,128)}, u32[]{:S(2)}) copy-start(f32[64,512]{1,0:T(8,128)} %start.1) | copy-start | bytes 393220
  9.4 10.1 %collective-permute-start.3 = (f32[2,4,32,128]{3,2,1,0:T(8,128)S(1)}, f32[2,4,32,128]{3,2,1,0:T(8,128)S(1)}, u32[]{:S(2)}, u32[]{:S(2)}) collective-permute-start(f32[2,4,32,128]{3,2,1,0:T(8,128)S(1)} %get-tuple-element.34), channel_id=1, source_target_pairs={{0,1},{1,0},{2,3},{3,2},{4,5},{5,4},{6,7},{7,6},{8,9},{9,8},{10,11... | collective-permute-start | bytes 393224 | tf_op jit(solution)/shard_map/late_near/ppermute | solution.py:405
  9.5 10.1 %collective-permute-start.4 = (f32[2,4,32,128]{3,2,1,0:T(8,128)S(1)}, f32[2,4,32,128]{3,2,1,0:T(8,128)S(1)}, u32[]{:S(2)}, u32[]{:S(2)}) collective-permute-start(f32[2,4,32,128]{3,2,1,0:T(8,128)S(1)} %get-tuple-element.35), channel_id=1, source_target_pairs={{1,2},{3,4},{5,6},{2,1},{4,3},{6,5},{9,10},{11,12},{13,14},{10,9},... | collective-permute-start | bytes 393224 | tf_op jit(solution)/shard_map/late_far/ppermute | solution.py:405
  13.7 5.9 %collective-permute-start.2 = (f32[2,2,4,48,128]{4,3,2,1,0:T(8,128)S(1)}, f32[2,2,4,48,128]{4,3,2,1,0:T(8,128)S(1)}, u32[]{:S(2)}, u32[]{:S(2)}) collective-permute-start(f32[2,2,4,48,128]{4,3,2,1,0:T(8,128)S(1)} %pad_maximum_fusion), channel_id=1, source_target_pairs={{0,8},{8,0},{16,24},{24,16},{1,9},{9,1},{17,25},{25,17},{2,10},{10... | collective-permute-start | bytes 1179656 | tf_op jit(solution)/shard_map/mates/ppermute | solution.py:405
  15.3 14.5 %collective-permute-start.8 = (f32[2,4,32,128]{3,2,1,0:T(8,128)S(1)}, f32[2,4,32,128]{3,2,1,0:T(8,128)S(1)}, u32[]{:S(2)}, u32[]{:S(2)}) collective-permute-start(f32[2,4,32,128]{3,2,1,0:T(8,128)S(1)} %get-tuple-element.44), channel_id=1, source_target_pairs={{0,1},{1,0},{2,3},{3,2},{4,5},{5,4},{6,7},{7,6},{8,9},{9,8},{10,11... | collective-permute-start | bytes 393224 | tf_op jit(solution)/shard_map/early_near/ppermute | solution.py:405
  15.3 14.5 %collective-permute-start.9 = (f32[2,4,32,128]{3,2,1,0:T(8,128)S(1)}, f32[2,4,32,128]{3,2,1,0:T(8,128)S(1)}, u32[]{:S(2)}, u32[]{:S(2)}) collective-permute-start(f32[2,4,32,128]{3,2,1,0:T(8,128)S(1)} %get-tuple-element.45), channel_id=1, source_target_pairs={{1,2},{3,4},{5,6},{2,1},{4,3},{6,5},{9,10},{11,12},{13,14},{10,9},... | collective-permute-start | bytes 393224 | tf_op jit(solution)/shard_map/early_far/ppermute | solution.py:405
  19.6 1.0 %copy-start.1 = (f32[4,4,64,128]{3,2,1,0:T(8,128)S(1)}, f32[4,4,64,128]{3,2,1,0:T(8,128)}, u32[]{:S(2)}) copy-start(f32[4,4,64,128]{3,2,1,0:T(8,128)} %get-tuple-element.30.mine) | copy-start | bytes 1572868
  26.0 12.3 %collective-permute-start.5 = (f32[2,4,48,128]{3,2,1,0:T(8,128)S(1)}, f32[2,4,48,128]{3,2,1,0:T(8,128)S(1)}, u32[]{:S(2)}, u32[]{:S(2)}) collective-permute-start(f32[2,4,48,128]{3,2,1,0:T(8,128)S(1)} %get-tuple-element.39), channel_id=1, source_target_pairs={{0,1},{1,0},{2,3},{3,2},{4,5},{5,4},{6,7},{7,6},{8,9},{9,8},{10,11... | collective-permute-start | bytes 589832 | tf_op jit(solution)/shard_map/late_settled_near/ppermute | solution.py:405
  26.1 12.2 %collective-permute-start.6 = (f32[2,4,48,128]{3,2,1,0:T(8,128)S(1)}, f32[2,4,48,128]{3,2,1,0:T(8,128)S(1)}, u32[]{:S(2)}, u32[]{:S(2)}) collective-permute-start(f32[2,4,48,128]{3,2,1,0:T(8,128)S(1)} %get-tuple-element.40), channel_id=1, source_target_pairs={{1,2},{3,4},{5,6},{2,1},{4,3},{6,5},{9,10},{11,12},{13,14},{10,9},... | collective-permute-start | bytes 589832 | tf_op jit(solution)/shard_map/late_settled_far/ppermute | solution.py:405
  34.8 14.1 %collective-permute-start.10 = (f32[2,4,48,128]{3,2,1,0:T(8,128)S(1)}, f32[2,4,48,128]{3,2,1,0:T(8,128)S(1)}, u32[]{:S(2)}, u32[]{:S(2)}) collective-permute-start(f32[2,4,48,128]{3,2,1,0:T(8,128)S(1)} %get-tuple-element.47), channel_id=1, source_target_pairs={{0,1},{1,0},{2,3},{3,2},{4,5},{5,4},{6,7},{7,6},{8,9},{9,8},{10,11... | collective-permute-start | bytes 589832 | tf_op jit(solution)/shard_map/early_settled_near/ppermute | solution.py:405
  34.9 14.0 %collective-permute-start.11 = (f32[2,4,48,128]{3,2,1,0:T(8,128)S(1)}, f32[2,4,48,128]{3,2,1,0:T(8,128)S(1)}, u32[]{:S(2)}, u32[]{:S(2)}) collective-permute-start(f32[2,4,48,128]{3,2,1,0:T(8,128)S(1)} %get-tuple-element.48), channel_id=1, source_target_pairs={{1,2},{3,4},{5,6},{2,1},{4,3},{6,5},{9,10},{11,12},{13,14},{10,9},... | collective-permute-start | bytes 589832 | tf_op jit(solution)/shard_map/early_settled_far/ppermute | solution.py:405
  45.5 10.4 %collective-permute-start.7 = (f32[4,240,128]{2,1,0:T(8,128)S(1)}, f32[4,240,128]{2,1,0:T(8,128)S(1)}, u32[]{:S(2)}, u32[]{:S(2)}) collective-permute-start(f32[4,240,128]{2,1,0:T(8,128)S(1)} %late_second_sweep.1), channel_id=1, source_target_pairs={{0,8},{8,16},{16,24},{24,0},{1,9},{9,17},{17,25},{25,1},{2,10},{10... | collective-permute-start | bytes 1474568 | tf_op jit(solution)/shard_map/next_slab/ppermute | solution.py:405
  56.9 11.3 %collective-permute-start.12 = (f32[1,4,32,128]{3,2,1,0:T(8,128)S(1)}, f32[1,4,32,128]{3,2,1,0:T(8,128)S(1)}, u32[]{:S(2)}, u32[]{:S(2)}) collective-permute-start(f32[1,4,32,128]{3,2,1,0:T(8,128)S(1)} %get-tuple-element.52), channel_id=1, source_target_pairs={{0,1},{1,0},{2,3},{3,2},{4,5},{5,4},{6,7},{7,6},{8,9},{9,8},{10,11... | collective-permute-start | bytes 196616 | tf_op jit(solution)/shard_map/slab_near/ppermute | solution.py:405
  57.0 11.2 %collective-permute-start.13 = (f32[1,4,32,128]{3,2,1,0:T(8,128)S(1)}, f32[1,4,32,128]{3,2,1,0:T(8,128)S(1)}, u32[]{:S(2)}, u32[]{:S(2)}) collective-permute-start(f32[1,4,32,128]{3,2,1,0:T(8,128)S(1)} %get-tuple-element.53), channel_id=1, source_target_pairs={{1,2},{3,4},{5,6},{2,1},{4,3},{6,5},{9,10},{11,12},{13,14},{10,9},... | collective-permute-start | bytes 196616 | tf_op jit(solution)/shard_map/slab_far/ppermute | solution.py:405

commit v3 on v2

--- a/solution.py
+++ b/solution.py
@@ -14,7 +14,6 @@
 PAD = 8
 NEAR = 16
 FINE = SUBSTEPS * COARSEN_ONE
-ALONE = 61 * 2**20
 VMEM_LIMIT = 24 * 2**20
 
 
@@ -26,16 +25,15 @@
     return [pl.BlockSpec(memory_space=pltpu.VMEM)] * count
 
 
-def call(kernel, name, outs, scratch, *arrays, cost=0, far=False, grant=VMEM_LIMIT):
-    held = [pl.BlockSpec(memory_space=pltpu.HBM)] * len(arrays) if far else vmem_specs(len(arrays))
+def call(kernel, name, outs, scratch, *arrays, cost=0):
     return pl.pallas_call(
         kernel,
         out_shape=[jax.ShapeDtypeStruct(shape, jnp.float32) for shape in outs],
-        in_specs=held,
+        in_specs=vmem_specs(len(arrays)),
         out_specs=vmem_specs(len(outs)),
         scratch_shapes=scratch,
         name=name,
-        compiler_params=pltpu.CompilerParams(vmem_limit_bytes=grant),
+        compiler_params=pltpu.CompilerParams(vmem_limit_bytes=VMEM_LIMIT),
         cost_estimate=pl.CostEstimate(flops=cost, bytes_accessed=1 << 20, transcendentals=0),
     )(*arrays)
 
@@ -126,41 +124,24 @@
         far[k] = source[k, :, pl.ds(high, width), :]
 
 
-def arrange(sources, homes, landed, arrivals, parts):
-    rows, columns = landed.shape[1:]
-    blocks = columns // LANES
-    copies = []
-    for k, choices in enumerate(sources):
-        made = [pltpu.make_async_copy(source, landed.at[k], arrivals.at[k]) for source in choices]
-        copies.append(made[-1])
-        if len(made) == 1:
-            made[0].start()
-        else:
-            pl.when(is_last_slab())(made[0].start)
-            pl.when(jnp.logical_not(is_last_slab()))(made[1].start)
-    order = column_order(columns, False)
-    for index, copy in enumerate(copies):
-        copy.wait()
-        for part, value in zip(parts, split_three(landed[index])):
+def arrange(fields, homes, parts):
+    count, rows, columns = fields.shape
+    for index in range(count):
+        for part, value in zip(parts, split_three(fields[index])):
             part[pl.ds(index * rows, rows), :] = value
-    result = reorder(parts, order)
+    result = reorder(parts, column_order(columns, False))
     for index, home in enumerate(homes):
-        for j in range(blocks):
+        for j in range(columns // LANES):
             home[j] = result[index * rows : (index + 1) * rows, j * LANES : (j + 1) * LANES]
 
 
-def coeffs_kernel(rate, along, across, drive, coeffs, share_near, share_far, landed, arrivals, *parts):
-    sources = [[rate], [along], [across], [drive]]
-    arrange(sources, [coeffs.at[k] for k in range(4)], landed, arrivals, parts)
+def coeffs_kernel(fields, coeffs, share_near, share_far, *parts):
+    arrange(fields, [coeffs.at[k] for k in range(4)], parts)
     sides(coeffs.at[pl.ds(2 * (lax.axis_index("tm") % 2), 2)], share_near, share_far)
 
 
-def points_kernel(
-    start, guessed, late, early, late_near, late_far, early_near, early_far, landed, arrivals, *parts
-):
-    sources = [[guessed.at[0]], [guessed.at[1]], [guessed.at[2]], [start, guessed.at[3]]]
-    homes = [early.at[0], early.at[1], late.at[0], late.at[1]]
-    arrange(sources, homes, landed, arrivals, parts)
+def points_kernel(fields, late, early, late_near, late_far, early_near, early_far, *parts):
+    arrange(fields, [early.at[0], early.at[1], late.at[0], late.at[1]], parts)
     sides(late, late_near, late_far)
     sides(early, early_near, early_far)
 
@@ -291,13 +272,13 @@
 
 
 def slab_kernel(raw, arrived, settled, swept, settled_last, e_out, c_out, c_near, c_far, coeffs, a, b):
-    kept = settled.shape[2]
     rows = settled_last.shape[2]
+    kept = rows + 2 * NEAR
     weights(raw, (raw.shape[2] - kept) // 2, coeffs, kept, float(COARSEN_ONE), False)
     for ref in (a, b):
         clear_ends(ref)
     inner = pl.ds(PAD, kept)
-    own = pl.ds(NEAR, rows)
+    own = pl.ds(NEAR // 2, rows)
     held = pl.ds(PAD + NEAR, rows)
     first, second, _ = moved(arrived, rows)
     trimmed = pl.ds(PAD + NEAR // 2, rows + NEAR)
@@ -306,10 +287,9 @@
     for position in range(1, COARSEN_TWO):
         coarse_step(a, b, coeffs, SUBSTEPS * (COARSEN_TWO - position), rows, 1)
         if position == 1:
-            value = second[...] - settled[0, :, pl.ds(NEAR // 2, rows + NEAR), :]
-            a[0, :, trimmed, :] = a[0, :, trimmed, :] + value
+            a[0, :, trimmed, :] = a[0, :, trimmed, :] + (second[...] - settled[0])
         elif position == 2:
-            a[0, :, inner, :] = a[0, :, inner, :] + (swept[0] - settled[1])
+            a[0, :, trimmed, :] = a[0, :, trimmed, :] + (swept[0] - settled[1])
         else:
             a[0, :, held, :] = a[0, :, held, :] + (swept[1, :, own, :] - settled_last[0])
         e_out[position] = a[0, :, held, :]
@@ -363,7 +343,7 @@
             if position == 0:
                 settled_here = moved(arrived, rows)[2]
             else:
-                settled_here = settled.at[position - 1, :, pl.ds(NEAR, rows), :]
+                settled_here = settled.at[position - 1, :, pl.ds(NEAR // 2, rows), :]
             value = x[0, :, held, :]
         else:
             settled_here = settled_last.at[0]
@@ -386,15 +366,16 @@
     field = (blocks, rows, LANES)
     wide_field = (blocks, FINE + NEAR, LANES)
     halo = (blocks, FINE, LANES)
-    landing = [pltpu.VMEM((4, rows, columns), jnp.float32), pltpu.SemaphoreType.DMA((4,))]
+    closing = jnp.where(is_last_slab(), start_field, guessed[points - 1])
+    fields = jnp.concatenate([guessed[: points - 1], closing[None]])
     parts = [pltpu.VMEM((4 * rows, columns), jnp.bfloat16)] * 3
     coeffs, share_near, share_far = call(
         coeffs_kernel, "arrange_coeffs", [(4,) + field] + [(2,) + wide_field] * 2,
-        landing + parts, diffusion, peclet_x, peclet_y, source, far=True, grant=ALONE,
+        parts, jnp.stack([diffusion, peclet_x, peclet_y, source]),
     )
     late, early, late_near, late_far, early_near, early_far = call(
         points_kernel, "arrange_points", [(2,) + field] * 2 + [(2,) + halo] * 4,
-        landing + parts, start_field, guessed, cost=2 * 10**9, far=True,
+        parts, fields, cost=2 * 10**9,
     )
     swap = [(i, i ^ 1) for i in range(strips)]
     cross = [(i, i + 1) for i in range(1, strips - 1, 2)] + [(i + 1, i) for i in range(1, strips - 1, 2)]
@@ -419,8 +400,9 @@
     window = (blocks, total + 2 * PAD, LANES)
     pair = [pltpu.VMEM((2,) + window, jnp.float32)] * 2
     work = 6 * 10**9
-    near = (2, blocks, rows + 2 * NEAR, LANES)
+    near = (2, blocks, rows + NEAR, LANES)
     sent = [(2,) + field] + [(2,) + wide_field] * 2
+    sent_early = [(2,) + field] + [(2, blocks, FINE + NEAR // 2, LANES)] * 2
     (loaded,) = call(window_kernel, "late_window", [(2,) + window], [], late, *late_sides, cost=10 * 10**9)
     fine, raw, late_settled, late_near, late_far = call(
         open_kernel, "late_first_sweep",
@@ -430,7 +412,7 @@
     )
     late_sides = exchange("late_settled", late_near, late_far)
     early_settled, early_near, early_far = call(
-        first_sweep, "early_first_sweep", sent, pair, fine, early, *early_sides, cost=work
+        first_sweep, "early_first_sweep", sent_early, pair, fine, early, *early_sides, cost=work
     )
     early_sides = exchange("early_settled", early_near, early_far)
     (outgoing,) = call(

time: 84.5 us -> 84.4 us (level)
  Pallas kernels: 37.8 us -> 33.7 us
  starting transfers between devices: 26.6 us -> 30.4 us
  local copies, waits for them, and re-layouts: 2.9 us -> 0.01 us
  other arithmetic: 0.04 us -> 1.31 us
  blocking collectives: 15 us -> 16.1 us
    pallas_call x9, Pallas kernels: 37.8 us -> 33.7 us  [call(): pl.pallas_call(kernel, out_shape=[jax.ShapeDtypeStruct(shape, jnp.float32...]
    ppermute x14, starting transfers between devices: 26.6 us -> 30.4 us  [send(): return lax.ppermute(value, axis, route)]
    unnamed x6 -> x4, local copies, waits for them, and re-layouts: 2.9 us -> 0.01 us
    another operation x0 -> x1, other arithmetic: none -> 1.22 us  [on_device(): jnp.stack([diffusion, peclet_x, peclet_y, source])]
    all_gather x1, blocking collectives: 7.68 us -> 8.78 us  [on_device(): gathered = lax.all_gather(c_value[0], 'tm')]
  transfers between devices with their start and end apart: 14 -> 14, of which waited for: 1 -> 1; matrix products, arithmetic and copies ran while one was open for 0% -> 0% of each run, Pallas kernels for 31% -> 29%
where the time goes in v3:
time: 84.4 us; the launch traced here: 83.1 us
  Pallas kernels  33.7 us (40%)
  starting transfers between devices  30.4 us (36%)
  blocking collectives  16.1 us (19%)
  other arithmetic  1.31 us (2%)
  waiting for transfers between devices  1.31 us (2%)
    pallas_call x9, Pallas kernels, call(): pl.pallas_call(kernel, out_shape=[jax.ShapeDtypeStruct(shape, jnp.float32...  33.7 us
    ppermute x14, starting transfers between devices, send(): return lax.ppermute(value, axis, route)  30.4 us
    all_gather x1, blocking collectives, on_device(): gathered = lax.all_gather(c_value[0], 'tm')  8.78 us
    all_gather x1, blocking collectives, on_device(): edges = lax.all_gather(jnp.concatenate(c_sides), 'tm')  7.29 us
  transfers between devices with their start and end apart: 14, of which 1 were waited for; matrix products, arithmetic and copies ran while one was open for 0% of the time, Pallas kernels for 29%

profile of v3, /device:TPU:25, one launch (start us, length us, event | category | flops | bytes accessed | tf_op | source)
XLA Modules:
  0.0 83.1 jit_solution(3222700039553956070)
XLA Ops:
  0.0 0.0 copy-start
  0.0 0.0 slice-start
  0.0 0.0 copy-start.1
  0.0 1.2 %pad_maximum_fusion.fields = f32[4,64,512]{2,1,0:T(8,128)S(1)} fusion(f32[1,64,512]{2,1,0:T(8,128)} %bitcast.16, f32[1,64,512]{2,1,0:T(8,128)} %bitcast.17, f32[1,64,512]{2,1,0:T(8,128)} %bitcast.18, f32[1,64,512]{2,1,0:T(8,128)} %bitcast.19), kind=kLoop, calls=%fused_computation | loop fusion | flops 393216 | bytes 1048576 | tf_op jit(solution)/shard_map/stack | solution.py:374
  1.2 0.6 arrange_coeffs.1
  1.9 1.3 %collective-permute-start = (f32[2,4,48,128]{3,2,1,0:T(8,128)S(1)}, f32[2,4,48,128]{3,2,1,0:T(8,128)S(1)}, u32[]{:S(2)}, u32[]{:S(2)}) collective-permute-start(f32[2,4,48,128]{3,2,1,0:T(8,128)S(1)} %get-tuple-element.31), channel_id=1, source_target_pairs={{0,1},{1,0},{2,3},{3,2},{4,5},{5,4},{6,7},{7,6},{8,9},{9,8},{10,11... | collective-permute-start | bytes 589832 | tf_op jit(solution)/shard_map/share_near/ppermute | solution.py:386
  3.1 2.0 %collective-permute-start.1 = (f32[2,4,48,128]{3,2,1,0:T(8,128)S(1)}, f32[2,4,48,128]{3,2,1,0:T(8,128)S(1)}, u32[]{:S(2)}, u32[]{:S(2)}) collective-permute-start(f32[2,4,48,128]{3,2,1,0:T(8,128)S(1)} %get-tuple-element.32), channel_id=1, source_target_pairs={{1,2},{3,4},{5,6},{2,1},{4,3},{6,5},{9,10},{11,12},{13,14},{10,9},... | collective-permute-start | bytes 589832 | tf_op jit(solution)/shard_map/share_far/ppermute | solution.py:386
  5.2 0.0 copy-done
  5.2 0.0 copy-done.1
  5.2 0.0 slice-done
  5.3 0.7 arrange_points.1
  5.9 0.1 collective-permute-start.3
  6.0 4.1 %collective-permute-start.4 = (f32[2,4,32,128]{3,2,1,0:T(8,128)S(1)}, f32[2,4,32,128]{3,2,1,0:T(8,128)S(1)}, u32[]{:S(2)}, u32[]{:S(2)}) collective-permute-start(f32[2,4,32,128]{3,2,1,0:T(8,128)S(1)} %get-tuple-element.35), channel_id=1, source_target_pairs={{1,2},{3,4},{5,6},{2,1},{4,3},{6,5},{9,10},{11,12},{13,14},{10,9},... | collective-permute-start | bytes 393224 | tf_op jit(solution)/shard_map/late_far/ppermute | solution.py:386
  10.2 0.0 collective-permute-done.share_near
  10.2 1.3 %collective-permute-done.1.share_far = f32[2,4,48,128]{3,2,1,0:T(8,128)S(1)} collective-permute-done((f32[2,4,48,128]{3,2,1,0:T(8,128)S(1)}, f32[2,4,48,128]{3,2,1,0:T(8,128)S(1)}, u32[]{:S(2)}, u32[]{:S(2)}) %collective-permute-start.1) | collective-permute-done | bytes 196640 | tf_op jit(solution)/shard_map/share_far/ppermute | solution.py:386
  11.5 4.9 %collective-permute-start.2 = (f32[2,2,4,48,128]{4,3,2,1,0:T(8,128)S(1)}, f32[2,2,4,48,128]{4,3,2,1,0:T(8,128)S(1)}, u32[]{:S(2)}, u32[]{:S(2)}) collective-permute-start(f32[2,2,4,48,128]{4,3,2,1,0:T(8,128)S(1)} %pad_maximum_fusion.2), channel_id=1, source_target_pairs={{0,8},{8,0},{16,24},{24,16},{1,9},{9,1},{17,25},{25,17},{2,10},{10... | collective-permute-start | bytes 1179656 | tf_op jit(solution)/shard_map/mates/ppermute | solution.py:386
  16.4 0.0 collective-permute-start.8
  16.4 4.0 %collective-permute-start.9 = (f32[2,4,32,128]{3,2,1,0:T(8,128)S(1)}, f32[2,4,32,128]{3,2,1,0:T(8,128)S(1)}, u32[]{:S(2)}, u32[]{:S(2)}) collective-permute-start(f32[2,4,32,128]{3,2,1,0:T(8,128)S(1)} %get-tuple-element.45), channel_id=1, source_target_pairs={{1,2},{3,4},{5,6},{2,1},{4,3},{6,5},{9,10},{11,12},{13,14},{10,9},... | collective-permute-start | bytes 393224 | tf_op jit(solution)/shard_map/early_far/ppermute | solution.py:386
  20.4 0.0 collective-permute-done.3.near
  20.4 0.0 collective-permute-done.4.far
  20.4 0.1 late_window.1.loaded
  20.5 0.0 collective-permute-done.2.mates
  20.5 5.4 %late_first_sweep.1 = (f32[6,4,176,128]{3,2,1,0:T(8,128)S(1)}, f32[3,4,128,128]{3,2,1,0:T(8,128)S(1)}, f32[2,4,64,128]{3,2,1,0:T(8,128)S(1)}, f32[2,4,48,128]{3,2,1,0:T(8,128)S(1)}, f32[2,4,48,128]{3,2,1,0:T(8,128)S(1)}) custom-call(f32[4,4,64,128]{3,2,1,0:T(8,128)S(1)} %get-tuple-element.30.mine, f32[2,4,48,128]{3,2,1,0:T(8,128)S(1)} %collective-permute-done.share_near, ...), custom_call_target="tpu_custom_call" | custom-call | flops 1000000000 | bytes 1048576 | tf_op jit(solution)/shard_map/late_first_sweep/pallas_call | solution.py:29
  25.9 0.1 collective-permute-start.5
  26.0 3.4 %collective-permute-start.6 = (f32[2,4,48,128]{3,2,1,0:T(8,128)S(1)}, f32[2,4,48,128]{3,2,1,0:T(8,128)S(1)}, u32[]{:S(2)}, u32[]{:S(2)}) collective-permute-start(f32[2,4,48,128]{3,2,1,0:T(8,128)S(1)} %get-tuple-element.40), channel_id=1, source_target_pairs={{1,2},{3,4},{5,6},{2,1},{4,3},{6,5},{9,10},{11,12},{13,14},{10,9},... | collective-permute-start | bytes 589832 | tf_op jit(solution)/shard_map/late_settled_far/ppermute | solution.py:386
  29.3 0.0 collective-permute-done.8.near
  29.4 0.0 collective-permute-done.9.far
  29.4 5.1 %early_first_sweep.1 = (f32[2,4,64,128]{3,2,1,0:T(8,128)S(1)}, f32[2,4,40,128]{3,2,1,0:T(8,128)S(1)}, f32[2,4,40,128]{3,2,1,0:T(8,128)S(1)}) custom-call(f32[6,4,176,128]{3,2,1,0:T(8,128)S(1)} %get-tuple-element.37.coeffs, f32[2,4,64,128]{3,2,1,0:T(8,128)S(1)} %get-tuple-element.41.own, f32[2,4,32,128]{3,2,1,0:T(8,128)S(1)} %collective-permute-done.8.near, ...), custom_call_target="tpu_custom_call" | custom-call | flops 6000000000 | bytes 1048576 | tf_op jit(solution)/shard_map/early_first_sweep/pallas_call | solution.py:29
  34.4 0.1 collective-permute-start.10
  34.5 4.3 %collective-permute-start.11 = (f32[2,4,40,128]{3,2,1,0:T(8,128)S(1)}, f32[2,4,40,128]{3,2,1,0:T(8,128)S(1)}, u32[]{:S(2)}, u32[]{:S(2)}) collective-permute-start(f32[2,4,40,128]{3,2,1,0:T(8,128)S(1)} %get-tuple-element.48), channel_id=1, source_target_pairs={{1,2},{3,4},{5,6},{2,1},{4,3},{6,5},{9,10},{11,12},{13,14},{10,9},... | collective-permute-start | bytes 491528 | tf_op jit(solution)/shard_map/early_settled_far/ppermute | solution.py:386
  38.8 0.0 collective-permute-done.5.near
  38.8 0.0 collective-permute-done.6.far
  38.8 7.0 %late_second_sweep.1 = f32[4,240,128]{2,1,0:T(8,128)S(1)} custom-call(f32[6,4,176,128]{3,2,1,0:T(8,128)S(1)} %get-tuple-element.37.coeffs, f32[2,4,64,128]{3,2,1,0:T(8,128)S(1)} %get-tuple-element.38.own.settled_last, f32[2,4,48,128]{3,2,1,0:T(8,128)S(1)} %collective-permute-done.5.near, f32[2,4,48,128]{3,2,1,0:T(8,128)S(1)} %collective-permute-done.6.far), custom_call_target="tpu_custom_call" | custom-call | flops 6000000000 | bytes 1048576 | tf_op jit(solution)/shard_map/late_second_sweep/pallas_call | solution.py:29
  45.8 2.8 %collective-permute-start.7 = (f32[4,240,128]{2,1,0:T(8,128)S(1)}, f32[4,240,128]{2,1,0:T(8,128)S(1)}, u32[]{:S(2)}, u32[]{:S(2)}) collective-permute-start(f32[4,240,128]{2,1,0:T(8,128)S(1)} %late_second_sweep.1), channel_id=1, source_target_pairs={{0,8},{8,16},{16,24},{24,0},{1,9},{9,17},{17,25},{25,1},{2,10},{10... | collective-permute-start | bytes 1474568 | tf_op jit(solution)/shard_map/next_slab/ppermute | solution.py:386
  48.6 0.0 collective-permute-done.10.near
  48.6 0.0 collective-permute-done.11.far
  48.6 5.9 %early_second_sweep.1 = (f32[2,4,80,128]{3,2,1,0:T(8,128)S(1)}, f32[2,4,80,128]{3,2,1,0:T(8,128)S(1)}) custom-call(f32[6,4,176,128]{3,2,1,0:T(8,128)S(1)} %get-tuple-element.37.coeffs, f32[2,4,64,128]{3,2,1,0:T(8,128)S(1)} %get-tuple-element.46.own, f32[2,4,40,128]{3,2,1,0:T(8,128)S(1)} %collective-permute-done.10.near, ...), custom_call_target="tpu_custom_call" | custom-call | flops 6000000000 | bytes 1048576 | tf_op jit(solution)/shard_map/early_second_sweep/pallas_call | solution.py:29
  54.6 0.0 collective-permute-done.7.arrived
  54.6 1.0 %slab_value.1 = (f32[4,4,64,128]{3,2,1,0:T(8,128)S(1)}, f32[1,4,64,128]{3,2,1,0:T(8,128)S(1)}, f32[1,4,32,128]{3,2,1,0:T(8,128)S(1)}, f32[1,4,32,128]{3,2,1,0:T(8,128)S(1)}) custom-call(f32[3,4,128,128]{3,2,1,0:T(8,128)S(1)} %get-tuple-element.36.raw, f32[4,240,128]{2,1,0:T(8,128)S(1)} %collective-permute-done.7.arrived, ...), custom_call_target="tpu_custom_call" | custom-call | bytes 1048576 | tf_op jit(solution)/shard_map/slab_value/pallas_call | solution.py:29
  55.6 0.1 collective-permute-start.12
  55.7 3.3 %collective-permute-start.13 = (f32[1,4,32,128]{3,2,1,0:T(8,128)S(1)}, f32[1,4,32,128]{3,2,1,0:T(8,128)S(1)}, u32[]{:S(2)}, u32[]{:S(2)}) collective-permute-start(f32[1,4,32,128]{3,2,1,0:T(8,128)S(1)} %get-tuple-element.53), channel_id=1, source_target_pairs={{1,2},{3,4},{5,6},{2,1},{4,3},{6,5},{9,10},{11,12},{13,14},{10,9},... | collective-permute-start | bytes 196616 | tf_op jit(solution)/shard_map/slab_far/ppermute | solution.py:386
  59.0 8.8 %all_gather.9.gathered = f32[4,4,64,128]{3,2,1,0:T(8,128)S(1)} all-gather(f32[1,4,64,128]{3,2,1,0:T(8,128)S(1)} %get-tuple-element.51), channel_id=1, replica_groups=mesh['tm'=4,'space'=8] {'tm'}, dimensions={0}, use_global_device_ids=true | all-gather | bytes 655360 | tf_op jit(solution)/shard_map/all_gather | solution.py:432
  67.8 0.0 collective-permute-done.12
  67.8 0.0 collective-permute-done.13
  67.8 7.3 %all-gather = f32[8,4,32,128]{3,2,1,0:T(8,128)S(1)} all-gather(f32[2,4,32,128]{3,2,1,0:T(8,128)S(1)} %pad_maximum_fusion.3), channel_id=2, replica_groups=mesh['tm'=4,'space'=8] {'tm'}, dimensions={0}, use_global_device_ids=true | all-gather | bytes 655360 | tf_op jit(solution)/shard_map/all_gather | solution.py:433
  75.1 7.9 %close.1 = f32[4,64,512]{2,1,0:T(8,128)} custom-call(f32[3,4,128,128]{3,2,1,0:T(8,128)S(1)} %get-tuple-element.36.raw, f32[4,4,64,128]{3,2,1,0:T(8,128)S(1)} %all_gather.9.gathered, f32[4,2,4,32,128]{4,3,2,1,0:T(8,128)S(1)} %bitcast.13, f32[4,240,128]{2,1,0:T(8,128)S(1)} %collective-permute-done.7.arrived, f32[2,4,80,128]{3,2,1,0:T(8,128)S(1)} %get-tuple-element.49.settled, ...), custom_call_target="tpu_custom_call" | custom-call | bytes 1048576 | tf_op jit(solution)/shard_map/close/pallas_call | solution.py:29
  (4 shorter events, 0.1 us)
Async XLA Ops:
  0.0 5.2 %copy-start = (f32[4,64,512]{2,1,0:T(8,128)S(1)}, f32[4,64,512]{2,1,0:T(8,128)}, u32[]{:S(2)}) copy-start(f32[4,64,512]{2,1,0:T(8,128)} %param.7) | copy-start | bytes 1572868
  0.0 5.2 %slice-start = ((f32[4,64,512]{2,1,0:T(8,128)}), f32[3,64,512]{2,1,0:T(8,128)S(1)}, s32[]{:S(2)}) async-start(f32[4,64,512]{2,1,0:T(8,128)} %param.7), calls=%async_computation | async-start | bytes 786432 | tf_op jit(solution)/shard_map/slice | solution.py:370
  0.0 5.2 %copy-start.1 = (f32[64,512]{1,0:T(8,128)S(1)}, f32[64,512]{1,0:T(8,128)}, u32[]{:S(2)}) copy-start(f32[64,512]{1,0:T(8,128)} %param.6) | copy-start | bytes 393220
  1.9 8.3 %collective-permute-start = (f32[2,4,48,128]{3,2,1,0:T(8,128)S(1)}, f32[2,4,48,128]{3,2,1,0:T(8,128)S(1)}, u32[]{:S(2)}, u32[]{:S(2)}) collective-permute-start(f32[2,4,48,128]{3,2,1,0:T(8,128)S(1)} %get-tuple-element.31), channel_id=1, source_target_pairs={{0,1},{1,0},{2,3},{3,2},{4,5},{5,4},{6,7},{7,6},{8,9},{9,8},{10,11... | collective-permute-start | bytes 589832 | tf_op jit(solution)/shard_map/share_near/ppermute | solution.py:386
  3.1 8.3 %collective-permute-start.1 = (f32[2,4,48,128]{3,2,1,0:T(8,128)S(1)}, f32[2,4,48,128]{3,2,1,0:T(8,128)S(1)}, u32[]{:S(2)}, u32[]{:S(2)}) collective-permute-start(f32[2,4,48,128]{3,2,1,0:T(8,128)S(1)} %get-tuple-element.32), channel_id=1, source_target_pairs={{1,2},{3,4},{5,6},{2,1},{4,3},{6,5},{9,10},{11,12},{13,14},{10,9},... | collective-permute-start | bytes 589832 | tf_op jit(solution)/shard_map/share_far/ppermute | solution.py:386
  5.9 14.4 %collective-permute-start.3 = (f32[2,4,32,128]{3,2,1,0:T(8,128)S(1)}, f32[2,4,32,128]{3,2,1,0:T(8,128)S(1)}, u32[]{:S(2)}, u32[]{:S(2)}) collective-permute-start(f32[2,4,32,128]{3,2,1,0:T(8,128)S(1)} %get-tuple-element.34), channel_id=1, source_target_pairs={{0,1},{1,0},{2,3},{3,2},{4,5},{5,4},{6,7},{7,6},{8,9},{9,8},{10,11... | collective-permute-start | bytes 393224 | tf_op jit(solution)/shard_map/late_near/ppermute | solution.py:386
  6.0 14.4 %collective-permute-start.4 = (f32[2,4,32,128]{3,2,1,0:T(8,128)S(1)}, f32[2,4,32,128]{3,2,1,0:T(8,128)S(1)}, u32[]{:S(2)}, u32[]{:S(2)}) collective-permute-start(f32[2,4,32,128]{3,2,1,0:T(8,128)S(1)} %get-tuple-element.35), channel_id=1, source_target_pairs={{1,2},{3,4},{5,6},{2,1},{4,3},{6,5},{9,10},{11,12},{13,14},{10,9},... | collective-permute-start | bytes 393224 | tf_op jit(solution)/shard_map/late_far/ppermute | solution.py:386
  11.5 9.0 %collective-permute-start.2 = (f32[2,2,4,48,128]{4,3,2,1,0:T(8,128)S(1)}, f32[2,2,4,48,128]{4,3,2,1,0:T(8,128)S(1)}, u32[]{:S(2)}, u32[]{:S(2)}) collective-permute-start(f32[2,2,4,48,128]{4,3,2,1,0:T(8,128)S(1)} %pad_maximum_fusion.2), channel_id=1, source_target_pairs={{0,8},{8,0},{16,24},{24,16},{1,9},{9,1},{17,25},{25,17},{2,10},{10... | collective-permute-start | bytes 1179656 | tf_op jit(solution)/shard_map/mates/ppermute | solution.py:386
  16.4 12.9 %collective-permute-start.8 = (f32[2,4,32,128]{3,2,1,0:T(8,128)S(1)}, f32[2,4,32,128]{3,2,1,0:T(8,128)S(1)}, u32[]{:S(2)}, u32[]{:S(2)}) collective-permute-start(f32[2,4,32,128]{3,2,1,0:T(8,128)S(1)} %get-tuple-element.44), channel_id=1, source_target_pairs={{0,1},{1,0},{2,3},{3,2},{4,5},{5,4},{6,7},{7,6},{8,9},{9,8},{10,11... | collective-permute-start | bytes 393224 | tf_op jit(solution)/shard_map/early_near/ppermute | solution.py:386
  16.4 12.9 %collective-permute-start.9 = (f32[2,4,32,128]{3,2,1,0:T(8,128)S(1)}, f32[2,4,32,128]{3,2,1,0:T(8,128)S(1)}, u32[]{:S(2)}, u32[]{:S(2)}) collective-permute-start(f32[2,4,32,128]{3,2,1,0:T(8,128)S(1)} %get-tuple-element.45), channel_id=1, source_target_pairs={{1,2},{3,4},{5,6},{2,1},{4,3},{6,5},{9,10},{11,12},{13,14},{10,9},... | collective-permute-start | bytes 393224 | tf_op jit(solution)/shard_map/early_far/ppermute | solution.py:386
  25.9 12.9 %collective-permute-start.5 = (f32[2,4,48,128]{3,2,1,0:T(8,128)S(1)}, f32[2,4,48,128]{3,2,1,0:T(8,128)S(1)}, u32[]{:S(2)}, u32[]{:S(2)}) collective-permute-start(f32[2,4,48,128]{3,2,1,0:T(8,128)S(1)} %get-tuple-element.39), channel_id=1, source_target_pairs={{0,1},{1,0},{2,3},{3,2},{4,5},{5,4},{6,7},{7,6},{8,9},{9,8},{10,11... | collective-permute-start | bytes 589832 | tf_op jit(solution)/shard_map/late_settled_near/ppermute | solution.py:386
  26.0 12.8 %collective-permute-start.6 = (f32[2,4,48,128]{3,2,1,0:T(8,128)S(1)}, f32[2,4,48,128]{3,2,1,0:T(8,128)S(1)}, u32[]{:S(2)}, u32[]{:S(2)}) collective-permute-start(f32[2,4,48,128]{3,2,1,0:T(8,128)S(1)} %get-tuple-element.40), channel_id=1, source_target_pairs={{1,2},{3,4},{5,6},{2,1},{4,3},{6,5},{9,10},{11,12},{13,14},{10,9},... | collective-permute-start | bytes 589832 | tf_op jit(solution)/shard_map/late_settled_far/ppermute | solution.py:386
  34.4 14.2 %collective-permute-start.10 = (f32[2,4,40,128]{3,2,1,0:T(8,128)S(1)}, f32[2,4,40,128]{3,2,1,0:T(8,128)S(1)}, u32[]{:S(2)}, u32[]{:S(2)}) collective-permute-start(f32[2,4,40,128]{3,2,1,0:T(8,128)S(1)} %get-tuple-element.47), channel_id=1, source_target_pairs={{0,1},{1,0},{2,3},{3,2},{4,5},{5,4},{6,7},{7,6},{8,9},{9,8},{10,11... | collective-permute-start | bytes 491528 | tf_op jit(solution)/shard_map/early_settled_near/ppermute | solution.py:386
  34.5 14.1 %collective-permute-start.11 = (f32[2,4,40,128]{3,2,1,0:T(8,128)S(1)}, f32[2,4,40,128]{3,2,1,0:T(8,128)S(1)}, u32[]{:S(2)}, u32[]{:S(2)}) collective-permute-start(f32[2,4,40,128]{3,2,1,0:T(8,128)S(1)} %get-tuple-element.48), channel_id=1, source_target_pairs={{1,2},{3,4},{5,6},{2,1},{4,3},{6,5},{9,10},{11,12},{13,14},{10,9},... | collective-permute-start | bytes 491528 | tf_op jit(solution)/shard_map/early_settled_far/ppermute | solution.py:386
  45.8 8.8 %collective-permute-start.7 = (f32[4,240,128]{2,1,0:T(8,128)S(1)}, f32[4,240,128]{2,1,0:T(8,128)S(1)}, u32[]{:S(2)}, u32[]{:S(2)}) collective-permute-start(f32[4,240,128]{2,1,0:T(8,128)S(1)} %late_second_sweep.1), channel_id=1, source_target_pairs={{0,8},{8,16},{16,24},{24,0},{1,9},{9,17},{17,25},{25,1},{2,10},{10... | collective-permute-start | bytes 1474568 | tf_op jit(solution)/shard_map/next_slab/ppermute | solution.py:386
  55.6 12.2 %collective-permute-start.12 = (f32[1,4,32,128]{3,2,1,0:T(8,128)S(1)}, f32[1,4,32,128]{3,2,1,0:T(8,128)S(1)}, u32[]{:S(2)}, u32[]{:S(2)}) collective-permute-start(f32[1,4,32,128]{3,2,1,0:T(8,128)S(1)} %get-tuple-element.52), channel_id=1, source_target_pairs={{0,1},{1,0},{2,3},{3,2},{4,5},{5,4},{6,7},{7,6},{8,9},{9,8},{10,11... | collective-permute-start | bytes 196616 | tf_op jit(solution)/shard_map/slab_near/ppermute | solution.py:386
  55.7 12.1 %collective-permute-start.13 = (f32[1,4,32,128]{3,2,1,0:T(8,128)S(1)}, f32[1,4,32,128]{3,2,1,0:T(8,128)S(1)}, u32[]{:S(2)}, u32[]{:S(2)}) collective-permute-start(f32[1,4,32,128]{3,2,1,0:T(8,128)S(1)} %get-tuple-element.53), channel_id=1, source_target_pairs={{1,2},{3,4},{5,6},{2,1},{4,3},{6,5},{9,10},{11,12},{13,14},{10,9},... | collective-permute-start | bytes 196616 | tf_op jit(solution)/shard_map/slab_far/ppermute | solution.py:386
